TPU v7x, 512 devices: a whole 4x4x16 slice. The times are simulated.
512 devices in a mesh: ens: 4 (over y_hi, core), lat: 32 (over z, y_lo), lon: 4 (over x).
Axes of the slice: x: 4, y: 4 (y_hi: 2, y_lo: 2; y = y_hi * 2 + y_lo), z: 16, core: 2. Of those that a mesh axis runs over, the one named last changes fastest.
Arguments:
- state_field: bfloat16 [4, 256, 64, 512], P('ens', None, 'lat', 'lon'), may hold values from -6 to 6
- first_weight: bfloat16 [3, 256, 256], replicated, may hold values from -0.21875 to 0.21875
- second_weight: bfloat16 [3, 256, 256], replicated, may hold values from -0.21875 to 0.21875
- quadrature: float32 [64, 3, 12], P('lat'), may hold values from 0.05 to 0.4
- lat_offsets: int32 [64, 3, 12], P('lat'), may hold values from -1 to 1, as said below
- lon_offsets: int32 [64, 3, 12], P('lat'), may hold values from -4 to 4, as said below
- cotangent: bfloat16 [4, 256, 64, 512], P('ens', None, 'lat', 'lon'), may hold values from -6 to 6
Outputs:
- layer_output: bfloat16 [4, 256, 64, 512], P('ens', None, 'lat', 'lon')
- state_grad: bfloat16 [4, 256, 64, 512], P('ens', None, 'lat', 'lon')
- first_grad: float32 [3, 256, 256], replicated
- second_grad: float32 [3, 256, 256], replicated
Inputs may be any that keep to these rules, and one draw needn't show every extreme that they name: `lat_offsets`: for every row and basis function the first three support points have latitude offsets 0, -1 and 1. `lon_offsets`: in a row p rows from the nearer pole the longitude offsets lie within plus or minus max(2, 4 - p), and the first three support points have offsets 0, minus that bound and that bound.
All inputs are finite; a program needn't handle non-finite values.
Results may differ from a plain program's by a relative error of at most 0.013.
Values may be sent and summed in bfloat16 or wider, within the bound.
A program may use at most 64 MiB of HBM per device.

v0:
```python
import math

import jax
import jax.numpy as jnp
from jax import lax
from jax.sharding import PartitionSpec as P

LAT_REACH = 1
LON_REACH = 4


def with_halo(block, sides, width, periodic):
    for axis, dim in sides:
        count = lax.axis_size(axis)
        forward = [(i, i + 1) for i in range(count - 1)]
        if periodic:
            forward.append((count - 1, 0))
        backward = [(target, source) for source, target in forward]
        low = lax.ppermute(
            lax.slice_in_dim(block, block.shape[dim] - width, None, axis=dim), axis, forward
        )
        high = lax.ppermute(lax.slice_in_dim(block, 0, width, axis=dim), axis, backward)
        block = jnp.concatenate([low, block, high], axis=dim)
    return block


def passed_along(value, axis, by):
    devices = lax.axis_size(axis)
    return lax.ppermute(value, axis, [(i, (i + by) % devices) for i in range(devices)])


def passed_along_2(value, axis, steps):
    count = lax.axis_size(axis)
    leading, last = (max(0, -steps), min(count, count - steps))
    return lax.ppermute(value, axis, [(source, source + steps) for source in range(leading, last)])


def coefficients(quadrature, lat_offsets, lon_offsets):
    lat_levels = jnp.arange(2 * LAT_REACH + 1, dtype=jnp.int32)
    lon_levels = jnp.arange(2 * LON_REACH + 1, dtype=jnp.int32)
    lat_onehot = (lat_offsets[..., None] + LAT_REACH == lat_levels).astype(jnp.float32)
    lon_onehot = (lon_offsets[..., None] + LON_REACH == lon_levels).astype(jnp.float32)
    stencil = jnp.einsum(
        "rks,rksa,rksd->krad", quadrature, lat_onehot, lon_onehot, precision=lax.Precision.HIGHEST
    )
    return stencil.astype(jnp.bfloat16)


def lon_picker(col_count):
    span_count = 2 * LON_REACH + 1
    wide_count = col_count + 2 * LON_REACH
    table_shape = (span_count, wide_count, col_count)
    offset_level = lax.broadcasted_iota(jnp.int32, table_shape, 0)
    source = lax.broadcasted_iota(jnp.int32, table_shape, 1)
    target = lax.broadcasted_iota(jnp.int32, table_shape, 2)
    matches = source - target == offset_level
    return matches.astype(jnp.bfloat16)


def widen(values):
    wide_lon = with_halo(values, (("lon", 2),), LON_REACH, True)
    return with_halo(wide_lon, (("lat", 1),), LAT_REACH, False)


def lon_pass(piece, steps):
    return passed_along(piece, "lon", steps)


def lat_pass(piece, steps):
    return passed_along_2(piece.astype(jnp.bfloat16), "lat", steps).astype(piece.dtype)


def mix_channels(weight, spreaded):
    return jnp.einsum("koc,cikj->oij", weight, spreaded, preferred_element_type=jnp.float32)


def filter_term(gradient, spreaded):
    return jnp.einsum("oij,cikj->koc", gradient, spreaded, preferred_element_type=jnp.float32)


def body(state_field, first_weight, second_weight, quadrature, lat_offsets, lon_offsets, cotangent):
    source = state_field[0]
    channels, row_count, col_count = source.shape
    lat_taps = 2 * LAT_REACH + 1
    wide_count = col_count + 2 * LON_REACH
    stencil = coefficients(quadrature, lat_offsets, lon_offsets)
    basis_count = stencil.shape[0]
    forward_band = jnp.einsum(
        "kiad,dpq->iapkq", stencil, lon_picker(col_count), preferred_element_type=jnp.float32
    )
    forward_band = forward_band.astype(jnp.bfloat16).reshape(
        row_count, lat_taps * wide_count, basis_count * col_count
    )

    def spread(values):
        extended = widen(values)
        stacked = jnp.stack(
            [extended[:, offset : offset + row_count] for offset in range(lat_taps)], axis=2
        )
        stacked = stacked.reshape(channels, row_count, lat_taps * wide_count)
        mixed = jnp.einsum(
            "cin,inm->cim", stacked, forward_band, preferred_element_type=jnp.float32
        )
        return mixed.reshape(channels, row_count, basis_count, col_count).astype(jnp.bfloat16)

    first_spread = spread(source)
    hidden = mix_channels(first_weight, first_spread)
    activation = jax.nn.gelu(hidden).astype(jnp.bfloat16)
    second_spread = spread(activation)
    layer_output = mix_channels(second_weight, second_spread).astype(jnp.bfloat16)
    gradient = cotangent[0]
    second_sum = filter_term(gradient, second_spread)

    def carry_back(weight, grad_rows):
        mixed_grad = jnp.einsum(
            "koc,oij->cikj", weight, grad_rows, preferred_element_type=jnp.float32
        ).astype(jnp.bfloat16)
        partial_rows = jnp.einsum(
            "cim,inm->cin",
            mixed_grad.reshape(channels, row_count, basis_count * col_count),
            forward_band,
            preferred_element_type=jnp.float32,
        )
        partial_rows = partial_rows.reshape(channels, row_count, lat_taps, wide_count)
        extended = jnp.zeros((channels, row_count + 2 * LAT_REACH, wide_count), jnp.float32)
        for offset in range(lat_taps):
            extended = extended + jnp.pad(
                partial_rows[:, :, offset], ((0, 0), (offset, lat_taps - 1 - offset), (0, 0))
            )
        left_rim = extended[:, :, :LON_REACH]
        right_rim = extended[:, :, LON_REACH + col_count :]
        core_block = extended[:, :, LON_REACH : LON_REACH + col_count]
        core_block = core_block.at[:, :, col_count - LON_REACH :].add(lon_pass(left_rim, -1))
        core_block = core_block.at[:, :, :LON_REACH].add(lon_pass(right_rim, 1))
        top_rows = core_block[:, :LAT_REACH]
        bottom_rows = core_block[:, LAT_REACH + row_count :]
        inner_rows = core_block[:, LAT_REACH : LAT_REACH + row_count]
        inner_rows = inner_rows.at[:, row_count - LAT_REACH :].add(lat_pass(top_rows, -1))
        inner_rows = inner_rows.at[:, :LAT_REACH].add(lat_pass(bottom_rows, 1))
        return inner_rows.astype(jnp.bfloat16)

    activation_grad = carry_back(second_weight, gradient)
    hidden_grad = jax.vjp(jax.nn.gelu, hidden)[1](activation_grad.astype(jnp.float32))[0].astype(
        jnp.bfloat16
    )
    first_sum = filter_term(hidden_grad, first_spread)
    state_grad = carry_back(first_weight, hidden_grad)
    first_sum, second_sum = lax.psum((first_sum, second_sum), ("ens", "lat", "lon"))
    member_total = state_field.shape[0] * lax.axis_size("ens")
    grad_scale = 1.0 / math.sqrt(
        member_total * row_count * lax.axis_size("lat") * col_count * lax.axis_size("lon")
    )
    return (layer_output[None], state_grad[None], first_sum * grad_scale, second_sum * grad_scale)


def solution(mesh):
    in_specs = (
        P("ens", None, "lat", "lon"),
        P(),
        P(),
        P("lat", None, None),
        P("lat", None, None),
        P("lat", None, None),
        P("ens", None, "lat", "lon"),
    )
    out_specs = (P("ens", None, "lat", "lon"), P("ens", None, "lat", "lon"), P(), P())
    return jax.shard_map(body, mesh=mesh, in_specs=in_specs, out_specs=out_specs, check_vma=False)
```

profile of v0, /device:TPU:1, one launch (start us, length us, event | category | flops | bytes accessed | tf_op | source)
XLA Modules:
  0.0 623.8 jit_solution(18057920773272051933)
XLA Ops:
  7.2 0.7 broadcast_add_fusion
  8.0 0.9 fusion.5
  8.9 0.6 fusion
  9.5 0.4 copy.50
  9.9 0.6 reshape.267
  10.4 0.4 copy-done.1
  11.2 0.4 fusion.48
  11.7 5.2 collective-permute-start.8
  16.9 1.9 collective-permute-start.9
  19.0 4.6 collective-permute-start.1
  23.5 1.9 collective-permute-start
  25.6 3.5 collective-permute-done
  29.2 3.2 collective-permute-start.2
  32.4 1.3 collective-permute-start.3
  33.8 1.3 collective-permute-start.10
  35.1 4.7 collective-permute-start.11
  40.0 0.4 convolution_convert_fusion.4
  40.4 1.3 collective-permute-done.11
  41.8 0.5 fusion.12
  42.3 1.9 collective-permute-start.5
  44.2 3.4 collective-permute-start.4
  47.9 0.4 fusion.49
  48.3 0.8 fusion.41
  49.5 1.2 copy.90
  50.7 0.7 pad_add_fusion
  51.4 1.1 fusion.40
  52.6 1.2 convolution_bitcast_fusion.1
  54.1 3.1 collective-permute-start.12
  57.2 2.2 collective-permute-start.13
  59.5 3.8 collective-permute-start.6
  63.3 1.3 collective-permute-start.7
  64.6 0.4 collective-permute-done.12
  65.2 42.8 %scatter-add.34 = f32[256,4,128]{2,1,0:T(4,128)S(1)} dynamic-update-slice(f32[256,4,128]{2,1,0:T(4,128)S(1)} %slice.353, f32[256,4,4]{2,1,0:T(4,128)S(1)} %slice_add_fusion.1, s32[]{:T(128)} %constant.204.clone.1, s32[]{:T(128)} %constant.204.clone.1, s32[]{:T(128)} %constant.205.clone.1) | dynamic-update-slice | bytes 32772 | tf_op jit(solution)/shard_map/scatter-add | solution.py:133
  108.1 8.4 %scatter-add.35 = f32[256,4,128]{2,1,0:T(4,128)S(1)} dynamic-update-slice(f32[256,4,128]{2,1,0:T(4,128)S(1)} %scatter-add.34, f32[256,4,4]{2,1,0:T(4,128)S(1)} %slice_add_fusion, s32[]{:T(128)} %constant.204.clone.1, s32[]{:T(128)} %constant.204.clone.1, s32[]{:T(128)} %constant.204.clone.1) | dynamic-update-slice | bytes 32772 | tf_op jit(solution)/shard_map/scatter-add | solution.py:134
  117.0 1.3 collective-permute-start.14
  118.3 5.5 collective-permute-start.15
  123.7 0.9 fusion.21
  124.8 0.4 convolution_convert_fusion.3
  125.2 0.4 copy-done.4
  125.6 1.2 convolution_bitcast_fusion
  127.2 0.8 copy.67
  128.2 2.9 scatter-add.36
  131.2 2.9 scatter-add.39
  134.1 0.7 convert_bitcast_fusion
  134.9 478.5 %all-reduce.9.cloned.1.call-done = (f32[3,256,256]{1,2,0:T(8,128)}, f32[3,256,256]{1,2,0:T(8,128)}) async-done(((f32[3,256,256]{1,2,0:T(8,128)}, f32[3,256,256]{1,2,0:T(8,128)}), (f32[3,256,256]{1,2,0:T(8,128)}, f32[3,256,256]{1,2,0:T(8,128)})) %all-reduce.9.cloned.1.call-update) | async-done | bytes 1572880 | tf_op jit(solution)/shard_map/psum | solution.py:148
  613.4 1.2 broadcast_multiply_fusion.1
  614.6 1.1 copy.68
  615.8 1.1 copy.69
  (66 shorter events, 3.7 us)
Async XLA Ops:
  7.2 34.6 %copy-start = (bf16[3,256,256]{2,1,0:T(8,128)(2,1)S(1)}, bf16[3,256,256]{2,1,0:T(8,128)(2,1)}, u32[]{:S(2)}) copy-start(bf16[3,256,256]{2,1,0:T(8,128)(2,1)} %param.24) | copy-start | bytes 1179652
  7.2 606.2 %all-reduce.9.cloned.1.call-start = ((), (), s32[]{:S(2)}) async-start(), calls=%async_computation | async-start | bytes 3145728 | tf_op jit(solution)/shard_map/psum | solution.py:148
  9.8 1.0 copy-start.1
  9.8 1.0 copy-start.3
  11.6 7.3 %copy-start.7 = (bf16[1,256,2,128]{3,2,1,0:T(2,128)(2,1)S(1)}, bf16[1,256,2,128]{3,2,1,0:T(2,128)(2,1)}, u32[]{:S(2)}) copy-start(bf16[1,256,2,128]{3,2,1,0:T(2,128)(2,1)} %param.23) | copy-start | bytes 393220
  11.7 22.0 %collective-permute-start.8 = (f32[256,4,4]{0,2,1:T(4,128)S(1)}, f32[256,4,4]{0,2,1:T(4,128)S(1)}, u32[]{:S(2)}, u32[]{:S(2)}) collective-permute-start(f32[256,4,4]{0,2,1:T(4,128)S(1)} %get-tuple-element.120), channel_id=1, source_target_pairs={{0,3},{1,0},{2,1},{3,2},{4,7},{5,4},{6,5},{7,6},{8,11},{9,8},{10,9... | collective-permute-start | bytes 49160 | tf_op jit(solution)/shard_map/ppermute | solution.py:29
  16.9 16.8 %collective-permute-start.9 = (f32[256,4,4]{0,2,1:T(4,128)S(1)}, f32[256,4,4]{0,2,1:T(4,128)S(1)}, u32[]{:S(2)}, u32[]{:S(2)}) collective-permute-start(f32[256,4,4]{0,2,1:T(4,128)S(1)} %get-tuple-element.119), channel_id=1, source_target_pairs={{0,1},{1,2},{2,3},{3,0},{4,5},{5,6},{6,7},{7,4},{8,9},{9,10},{10,1... | collective-permute-start | bytes 49160 | tf_op jit(solution)/shard_map/ppermute | solution.py:29
  19.0 6.6 %collective-permute-start.1 = (bf16[256,2,4]{0,2,1:T(4,128)(2,1)S(1)}, bf16[256,2,4]{0,2,1:T(4,128)(2,1)S(1)}, u32[]{:S(2)}, u32[]{:S(2)}) collective-permute-start(bf16[256,2,4]{0,2,1:T(4,128)(2,1)S(1)} %get-tuple-element.143), channel_id=1, source_target_pairs={{1,0},{2,1},{3,2},{0,3},{5,4},{6,5},{7,6},{4,7},{9,8},{10,9},{11,1... | collective-permute-start | bytes 12296 | tf_op jit(solution)/shard_map/ppermute | solution.py:22
  23.5 5.6 collective-permute-start
  29.2 10.7 %collective-permute-start.2 = (bf16[256,1,136]{0,2,1:T(8,128)(2,1)S(1)}, bf16[256,1,136]{0,2,1:T(8,128)(2,1)S(1)}, u32[]{:S(2)}, u32[]{:S(2)}) collective-permute-start(bf16[256,1,136]{0,2,1:T(8,128)(2,1)S(1)} %get-tuple-element.138), channel_id=1, source_target_pairs={{0,4},{4,8},{8,12},{12,16},{16,20},{20,24},{24,28},{28,32},{32,36}... | collective-permute-start | bytes 208904 | tf_op jit(solution)/shard_map/ppermute | solution.py:19
  32.4 7.5 %collective-permute-start.3 = (bf16[256,1,136]{0,2,1:T(8,128)(2,1)S(1)}, bf16[256,1,136]{0,2,1:T(8,128)(2,1)S(1)}, u32[]{:S(2)}, u32[]{:S(2)}) collective-permute-start(bf16[256,1,136]{0,2,1:T(8,128)(2,1)S(1)} %get-tuple-element.139), channel_id=1, source_target_pairs={{4,0},{8,4},{12,8},{16,12},{20,16},{24,20},{28,24},{32,28},{36,32}... | collective-permute-start | bytes 208904 | tf_op jit(solution)/shard_map/ppermute | solution.py:22
  33.8 6.6 %collective-permute-start.10 = (bf16[256,1,128]{0,2,1:T(8,128)(2,1)S(1)}, bf16[256,1,128]{0,2,1:T(8,128)(2,1)S(1)}, u32[]{:S(2)}, u32[]{:S(2)}) collective-permute-start(bf16[256,1,128]{0,2,1:T(8,128)(2,1)S(1)} %get-tuple-element.129), channel_id=1, source_target_pairs={{4,0},{8,4},{12,8},{16,12},{20,16},{24,20},{28,24},{32,28},{36,32}... | collective-permute-start | bytes 196616 | tf_op jit(solution)/shard_map/ppermute | solution.py:35
  35.1 6.6 %collective-permute-start.11 = (bf16[256,1,128]{0,2,1:T(8,128)(2,1)S(1)}, bf16[256,1,128]{0,2,1:T(8,128)(2,1)S(1)}, u32[]{:S(2)}, u32[]{:S(2)}) collective-permute-start(bf16[256,1,128]{0,2,1:T(8,128)(2,1)S(1)} %get-tuple-element.128), channel_id=1, source_target_pairs={{0,4},{4,8},{8,12},{12,16},{16,20},{20,24},{24,28},{28,32},{32,36}... | collective-permute-start | bytes 196616 | tf_op jit(solution)/shard_map/ppermute | solution.py:35
  42.3 6.0 copy-start.5
  42.3 17.1 %collective-permute-start.5 = (bf16[256,2,4]{0,2,1:T(4,128)(2,1)S(1)}, bf16[256,2,4]{0,2,1:T(4,128)(2,1)S(1)}, u32[]{:S(2)}, u32[]{:S(2)}) collective-permute-start(bf16[256,2,4]{0,2,1:T(4,128)(2,1)S(1)} %get-tuple-element.141), channel_id=1, source_target_pairs={{1,0},{2,1},{3,2},{0,3},{5,4},{6,5},{7,6},{4,7},{9,8},{10,9},{11,1... | collective-permute-start | bytes 12296 | tf_op jit(solution)/shard_map/ppermute | solution.py:22
  44.2 15.2 %collective-permute-start.4 = (bf16[256,2,4]{0,2,1:T(4,128)(2,1)S(1)}, bf16[256,2,4]{0,2,1:T(4,128)(2,1)S(1)}, u32[]{:S(2)}, u32[]{:S(2)}) collective-permute-start(bf16[256,2,4]{0,2,1:T(4,128)(2,1)S(1)} %get-tuple-element.140), channel_id=1, source_target_pairs={{0,1},{1,2},{2,3},{3,0},{4,5},{5,6},{6,7},{7,4},{8,9},{9,10},{10,1... | collective-permute-start | bytes 12296 | tf_op jit(solution)/shard_map/ppermute | solution.py:19
  51.4 1.2 copy-start.6
  54.1 10.9 %collective-permute-start.12 = (f32[256,4,4]{2,1,0:T(4,128)S(1)}, f32[256,4,4]{2,1,0:T(4,128)S(1)}, u32[]{:S(2)}, u32[]{:S(2)}) collective-permute-start(f32[256,4,4]{2,1,0:T(4,128)S(1)} %get-tuple-element.115), channel_id=1, source_target_pairs={{0,3},{1,0},{2,1},{3,2},{4,7},{5,4},{6,5},{7,6},{8,11},{9,8},{10,9... | collective-permute-start | bytes 49160 | tf_op jit(solution)/shard_map/ppermute | solution.py:29
  57.2 50.7 %collective-permute-start.13 = (f32[256,4,4]{2,1,0:T(4,128)}, f32[256,4,4]{2,1,0:T(4,128)S(1)}, u32[]{:S(2)}, u32[]{:S(2)}) collective-permute-start(f32[256,4,4]{2,1,0:T(4,128)} %get-tuple-element.114), channel_id=1, source_target_pairs={{0,1},{1,2},{2,3},{3,0},{4,5},{5,6},{6,7},{7,4},{8,9},{9,10},{10,1... | collective-permute-start | bytes 49160 | tf_op jit(solution)/shard_map/ppermute | solution.py:29
  59.5 64.2 %collective-permute-start.6 = (bf16[256,1,136]{0,2,1:T(8,128)(2,1)S(1)}, bf16[256,1,136]{0,2,1:T(8,128)(2,1)S(1)}, u32[]{:S(2)}, u32[]{:S(2)}) collective-permute-start(bf16[256,1,136]{0,2,1:T(8,128)(2,1)S(1)} %get-tuple-element.133), channel_id=1, source_target_pairs={{0,4},{4,8},{8,12},{12,16},{16,20},{20,24},{24,28},{28,32},{32,36}... | collective-permute-start | bytes 208904 | tf_op jit(solution)/shard_map/ppermute | solution.py:19
  63.3 60.4 %collective-permute-start.7 = (bf16[256,1,136]{0,2,1:T(8,128)(2,1)S(1)}, bf16[256,1,136]{0,2,1:T(8,128)(2,1)}, u32[]{:S(2)}, u32[]{:S(2)}) collective-permute-start(bf16[256,1,136]{0,2,1:T(8,128)(2,1)S(1)} %get-tuple-element.134), channel_id=1, source_target_pairs={{4,0},{8,4},{12,8},{16,12},{20,16},{24,20},{28,24},{32,28},{36,32}... | collective-permute-start | bytes 208904 | tf_op jit(solution)/shard_map/ppermute | solution.py:22
  117.0 11.0 %collective-permute-start.14 = (bf16[256,1,128]{2,1,0:T(2,128)(2,1)S(1)}, bf16[256,1,128]{2,1,0:T(2,128)(2,1)S(1)}, u32[]{:S(2)}, u32[]{:S(2)}) collective-permute-start(bf16[256,1,128]{2,1,0:T(2,128)(2,1)S(1)} %get-tuple-element.125), channel_id=1, source_target_pairs={{4,0},{8,4},{12,8},{16,12},{20,16},{24,20},{28,24},{32,28},{36,32}... | collective-permute-start | bytes 196616 | tf_op jit(solution)/shard_map/ppermute | solution.py:35
  118.3 12.8 %collective-permute-start.15 = (bf16[256,1,128]{2,1,0:T(2,128)(2,1)S(1)}, bf16[256,1,128]{2,1,0:T(2,128)(2,1)S(1)}, u32[]{:S(2)}, u32[]{:S(2)}) collective-permute-start(bf16[256,1,128]{2,1,0:T(2,128)(2,1)S(1)} %get-tuple-element.124), channel_id=1, source_target_pairs={{0,4},{4,8},{8,12},{12,16},{16,20},{20,24},{24,28},{28,32},{32,36}... | collective-permute-start | bytes 196616 | tf_op jit(solution)/shard_map/ppermute | solution.py:35
  124.7 0.9 copy-start.4
  614.6 1.2 copy-start.2
Sparse Core Ops, SparseCore 0:
  127.0 486.3 all-reduce.8
where the time goes:
time: 625 us; the launch traced here: 624 us
  waiting for transfers between devices  484 us (77%)
  local copies, waits for them, and re-layouts  66.4 us (11%)
  starting transfers between devices  46.5 us (7%)
  between operations  14.7 us (2%)
  matrix products  6.82 us (1%)
    psum x1, waiting for transfers between devices, body(): lax.psum((first_sum, second_sum), ('ens', 'lat', 'lon'))  478 us
    scatter-add x1, local copies, waits for them, and re-layouts, carry_back(): core_block.at[:, :, col_count - LON_REACH:].add(lon_pass(left_rim, -1))  42.8 us
    ppermute x4, starting transfers between devices, passed_along_2(): lax.ppermute(value, axis, [(source, source + steps) for source in range(l...  12.7 us
  transfers between devices with their start and end apart: 17, of which 4 were waited for; matrix products, arithmetic and copies ran while one was open for 11% of the time, Pallas kernels for 0%

commit v1 on v0

v1 whole, which is shorter than its diff:
```python
import math

import jax
import jax.numpy as jnp
from jax import lax
from jax.experimental import pallas as pl
from jax.experimental.pallas import tpu as pltpu
from jax.sharding import PartitionSpec as P

MESH = pl.DeviceIdType.MESH
BF = jnp.bfloat16
F32 = jnp.float32

PIECE = 96


def dot(a, b, ca, cb):
    return lax.dot_general(a, b, (((ca,), (cb,)), ((), ())), preferred_element_type=F32)


def copy_to(src, dst, send, recv, device):
    return pltpu.make_async_remote_copy(
        src_ref=src, dst_ref=dst, send_sem=send, recv_sem=recv, device_id=device, device_id_type=MESH
    )


def tap_rows(quad, lat_off, lon_off, a, sign):
    lane = lax.broadcasted_iota(jnp.int32, (3, 128), 1)
    offset = jnp.where(lane < 64, lane, lane - 128) * sign
    total = jnp.zeros((3, 128), F32)
    for s in range(12):
        hit = (lon_off[:, s : s + 1] == offset) & (lat_off[:, s : s + 1] == a - 1)
        total = total + jnp.where(hit, quad[:, s : s + 1], 0.0)
    return total.astype(BF).astype(F32)


def banded(row, count, first, shift):
    wide = jnp.broadcast_to(row, (count, 128))
    return pltpu.roll(wide, (shift + first) % 128, 1, stride=1, stride_axis=0)


def main_band(row):
    block = banded(row, 128, 0, 0)
    gap = lax.broadcasted_iota(jnp.int32, (128, 128), 1) - lax.broadcasted_iota(jnp.int32, (128, 128), 0)
    return jnp.where((gap <= 4) & (gap >= -4), block, 0.0).astype(BF)


def edge_band(rows_of, first):
    total = jnp.zeros((16, 128), F32)
    lane = lax.broadcasted_iota(jnp.int32, (16, 128), 1)
    cell = lax.broadcasted_iota(jnp.int32, (16, 128), 0) + first
    for place, row in rows_of:
        t = lane - 32 * place
        block = banded(row, 16, first, 32 * place + 16)
        gap = jnp.where(t < 16, t - 16, t + 112) - cell
        ok = (t >= 0) & (t < 32) & (gap <= 4) & (gap >= -4)
        total = total + jnp.where(ok, block, 0.0)
    return total.astype(BF)


def kernel(
    x_ref, g_ref, w1_ref, w2_ref, quad_ref, lato_ref, lono_ref,
    lo_ref, sg_ref, d1_ref, d2_ref,
    ext1, ext2, bsend, brecv, bandf, banda, u_ref, t_ref, slope,
    gs, crecv, xs, xrecv, zrecv, zgroup, fin,
    s1, r1, s2, r2, sc, rc, sx, rx, sz, rz, sf, rf, sa, ra, sd, rd,
):
    e, l, x = lax.axis_index("ens"), lax.axis_index("lat"), lax.axis_index("lon")
    yh, core = e // 2, e % 2
    z, yl = l // 2, l % 2
    y = yh * 2 + yl
    me = y * 4 + x
    p, grp = z % 4, z // 4
    up, down = (l + 31) % 32, (l + 1) % 32
    left, right = (x + 3) % 4, (x + 1) % 4
    partner = (yh * 2 + 1 - core, l, x)

    def xy_peer(s):
        xx, yy = (x + s % 4) % 4, (y + s // 4) % 4
        return yy * 4 + xx, ((yy // 2) * 2 + core, z * 2 + yy % 2, xx)

    def z_device(zz):
        return (e, zz * 2 + yl, x)

    barrier = pltpu.get_barrier_semaphore()

    def hello(device):
        pl.semaphore_signal(barrier, inc=1, device_id=device, device_id_type=MESH)

    for ll, xx in ((up, x), (down, x), (l, left), (l, right), (up, left), (up, right), (down, left), (down, right)):
        hello((e, ll, xx))
    hello(partner)

    def hello_xy(s, c):
        hello(xy_peer(s)[1])
        return c

    lax.fori_loop(1, 16, hello_xy, 0)

    def hello_z(s, c):
        hello(z_device((z + s) % 16))
        return c

    lax.fori_loop(1, 16, hello_z, 0)

    ext1[0, 1:3] = x_ref[...].reshape(2, 4, 32, 256)
    ext1[1, 1:3] = g_ref[...].reshape(2, 4, 32, 256)
    taps = [(quad_ref[i], lato_ref[i], lono_ref[i]) for i in range(2)]
    adj = [[tap_rows(*taps[i], a, -1) for a in range(3)] for i in range(2)]
    bsend[...] = jnp.zeros((2, 8, 128), F32)
    bsend[0, 0:3] = adj[0][0]
    bsend[1, 0:3] = adj[1][2]

    pl.semaphore_wait(barrier, 8 + 1 + 15 + 15)

    first = [
        copy_to(bsend.at[0], brecv.at[1], s1.at[0], r1.at[0], (e, up, x)),
        copy_to(bsend.at[1], brecv.at[0], s1.at[1], r1.at[1], (e, down, x)),
        copy_to(ext1.at[0, 1], ext1.at[0, 4], s1.at[2], r1.at[2], (e, up, x)),
        copy_to(ext1.at[0, 2], ext1.at[0, 0], s1.at[3], r1.at[3], (e, down, x)),
    ]

    def edges(ext, s, r, n):
        return [
            copy_to(ext.at[:, 1:3, 3, 16:32], ext.at[:, 3, 1:3, 0:16], s.at[n], r.at[n], (e, l, right)),
            copy_to(ext.at[:, 1:3, 0, 0:16], ext.at[:, 3, 1:3, 16:32], s.at[n + 1], r.at[n + 1], (e, l, left)),
            copy_to(ext.at[:, 2, 3, 16:32], ext.at[:, 3, 0, 0:16], s.at[n + 2], r.at[n + 2], (e, down, right)),
            copy_to(ext.at[:, 2, 0, 0:16], ext.at[:, 3, 0, 16:32], s.at[n + 3], r.at[n + 3], (e, down, left)),
            copy_to(ext.at[:, 1, 3, 16:32], ext.at[:, 3, 3, 0:16], s.at[n + 4], r.at[n + 4], (e, up, right)),
            copy_to(ext.at[:, 1, 0, 0:16], ext.at[:, 3, 3, 16:32], s.at[n + 5], r.at[n + 5], (e, up, left)),
        ]

    first += edges(ext1, s1, r1, 6)
    first += [
        copy_to(ext1.at[1, 1], ext1.at[1, 4], s1.at[4], r1.at[4], (e, up, x)),
        copy_to(ext1.at[1, 2], ext1.at[1, 0], s1.at[5], r1.at[5], (e, down, x)),
    ]
    for c in first:
        c.start()

    top, bottom = (l > 0).astype(F32), (l < 31).astype(F32)
    col = ((0, 1, 2, 3), (0, 1, 3, 2))

    def put_bands(band, i, rows):
        for k in range(3):
            out = slice(k * 128, k * 128 + 128)
            for n in range(3):
                c = col[i][n] * 128
                band[i, out, c : c + 128] = main_band(rows[n][k : k + 1])
            c = col[i][3] * 128
            places = [(i + n, rows[n][k : k + 1]) for n in range(3)]
            band[i, k * 128 : k * 128 + 16, c : c + 128] = edge_band(places, 0)
            band[i, k * 128 + 16 : k * 128 + 112, c : c + 128] = jnp.zeros((96, 128), BF)
            band[i, k * 128 + 112 : k * 128 + 128, c : c + 128] = edge_band(places, 112)

    fwd = [[tap_rows(*taps[i], a, 1) for a in range(3)] for i in range(2)]
    put_bands(bandf, 0, [fwd[0][0] * top, fwd[0][1], fwd[0][2]])
    put_bands(bandf, 1, [fwd[1][0], fwd[1][1], fwd[1][2] * bottom])
    first[0].wait_recv()
    first[1].wait_recv()
    put_bands(banda, 0, [brecv[0, 0:3] * top, adj[0][1], adj[1][0]])
    put_bands(banda, 1, [adj[0][2], adj[1][1], brecv[1, 0:3] * bottom])

    def spread(band, ext, f, out):
        for i in range(2):
            cells = ext[f, i : i + 4].reshape(512, 256)
            got = dot(band[i], cells, 1, 0).astype(BF)
            for k in range(3):
                out[k, i * 128 : i * 128 + 128] = got[k * 128 : k * 128 + 128]

    def mixed(spreaded, weight, cw):
        total = dot(spreaded[0], weight[0], 1, cw)
        for k in range(1, 3):
            total = total + dot(spreaded[k], weight[k], 1, cw)
        return total

    for c in first[2:10]:
        c.wait_recv()
    spread(bandf, ext1, 0, u_ref)
    hidden = mixed(u_ref, w1_ref, 1)
    root = math.sqrt(2.0 / math.pi)
    square = hidden * hidden
    bend = jnp.tanh(root * hidden * (1.0 + 0.044715 * square))
    act = (0.5 * hidden * (1.0 + bend)).astype(BF)
    slope[...] = 0.5 * (1.0 + bend) + (0.5 * root) * hidden * (1.0 - bend * bend) * (1.0 + (3 * 0.044715) * square)
    ext2[0, 1:3] = act.reshape(2, 4, 32, 256)
    second = [
        copy_to(ext2.at[0, 1], ext2.at[0, 4], s2.at[0], r2.at[0], (e, up, x)),
        copy_to(ext2.at[0, 2], ext2.at[0, 0], s2.at[1], r2.at[1], (e, down, x)),
        copy_to(ext2.at[1, 1], ext2.at[1, 4], s2.at[2], r2.at[2], (e, up, x)),
        copy_to(ext2.at[1, 2], ext2.at[1, 0], s2.at[3], r2.at[3], (e, down, x)),
    ]
    second += edges(ext2, s2, r2, 4)
    second[0].start()
    second[1].start()

    first[10].wait_recv()
    first[11].wait_recv()
    spread(banda, ext1, 1, t_ref)

    def put_grad(row, value):
        value = value.astype(BF)
        gs[0, row : row + 256] = value[:, :128]
        gs[1, row : row + 256] = value[:, 128:]

    for k in range(3):
        put_grad(768 + k * 256, dot(t_ref[k], act, 0, 0))
    core2 = copy_to(gs.at[1 - core, 768:1536], crecv.at[768:1536], sc.at[0], rc.at[0], partner)
    core2.start()
    act_grad = mixed(t_ref, w2_ref, 0).astype(BF).astype(F32)
    hid_grad = (act_grad * slope[...]).astype(BF)
    ext2[1, 1:3] = hid_grad.reshape(2, 4, 32, 256)
    for k in range(3):
        put_grad(k * 256, dot(hid_grad, u_ref[k], 0, 0))
    core1 = copy_to(gs.at[1 - core, 0:768], crecv.at[0:768], sc.at[1], rc.at[1], partner)
    core1.start()

    core2.wait_recv()
    xs[768:1536] = (gs[core, 768:1536].astype(F32) + crecv[768:1536].astype(F32)).astype(BF)
    core1.wait_recv()
    xs[0:768] = (gs[core, 0:768].astype(F32) + crecv[0:768].astype(F32)).astype(BF)

    def piece(s):
        peer, device = xy_peer(s)
        rows = pl.ds(pl.multiple_of(peer * PIECE, 16), PIECE)
        return copy_to(xs.at[rows], xrecv.at[s - 1], sx.at[s - 1], rx.at[s - 1], device)

    def send_piece(s, c):
        piece(s).start()
        return c

    lax.fori_loop(1, 16, send_piece, 0)
    for c in second[2:]:
        c.start()

    mine = pl.ds(pl.multiple_of(me * PIECE, 16), PIECE)

    def add_piece(s, total):
        piece(s).wait_recv()
        return total + xrecv[s - 1].astype(F32)

    total = lax.fori_loop(1, 16, add_piece, xs[mine].astype(F32))
    zrecv[p] = total.astype(BF)

    def near(s):
        return copy_to(zrecv.at[p], zrecv.at[p], sz.at[s - 1], rz.at[p], z_device(grp * 4 + (p + s) % 4))

    def near_in(s):
        q = (p + s) % 4
        return copy_to(zrecv.at[q], zrecv.at[q], sz.at[s - 1], rz.at[q], z_device(grp * 4 + q))

    for s in range(1, 4):
        near(s).start()

    for n in (0, 1, 4, 5, 6, 7, 8, 9):
        second[n].wait_recv()
    core2.wait_send()
    core1.wait_send()
    for c in first:
        c.wait_send()
    for s in range(1, 4):
        near_in(s).wait_recv()
    total = zrecv[0].astype(F32)
    for q in range(1, 4):
        total = total + zrecv[q].astype(F32)
    zgroup[grp] = total.astype(BF)

    def far(n, group, member):
        return copy_to(zgroup.at[grp], zgroup.at[grp], sf.at[n], rf.at[grp], z_device(group * 4 + member))

    to_left = [((grp + 3) % 4, 3), ((grp + 3) % 4, 2), ((grp + 3) % 4, 1), ((grp + 3) % 4, 0), ((grp + 2) % 4, 3), ((grp + 2) % 4, 2)]
    to_right = [((grp + 1) % 4, 0), ((grp + 1) % 4, 1), ((grp + 1) % 4, 2), ((grp + 1) % 4, 3), ((grp + 2) % 4, 0), ((grp + 2) % 4, 1)]

    @pl.when(p == 0)
    def _():
        for n in (4, 5, 3, 2, 1, 0):
            far(n, *to_left[n]).start()

    @pl.when(p == 3)
    def _():
        for n in (4, 5, 3, 2, 1, 0):
            far(n, *to_right[n]).start()

    spread(bandf, ext2, 0, u_ref)
    lo_ref[...] = mixed(u_ref, w2_ref, 1).astype(BF)
    second[2].wait_recv()
    second[3].wait_recv()
    spread(banda, ext2, 1, t_ref)
    sg_ref[...] = mixed(t_ref, w1_ref, 0).astype(BF)

    for s in range(1, 4):
        q = (grp + s) % 4
        copy_to(zgroup.at[q], zgroup.at[q], sf.at[0], rf.at[q], z_device(q * 4)).wait_recv()
    total = zgroup[0].astype(F32)
    for q in range(1, 4):
        total = total + zgroup[q].astype(F32)
    fin[core, mine] = total.astype(BF)

    def spread_piece(s):
        return copy_to(fin.at[core, mine], fin.at[core, mine], sa.at[s - 1], ra.at[s - 1], xy_peer(s)[1])

    def send_back(s, c):
        spread_piece(s).start()
        return c

    lax.fori_loop(1, 16, send_back, 0)

    def wait_back(s, c):
        spread_piece(s).wait_recv()
        return c

    lax.fori_loop(1, 16, wait_back, 0)
    swap = copy_to(fin.at[core], fin.at[core], sd.at[0], rd.at[0], partner)
    swap.start()

    for c in second:
        c.wait_send()

    def wait_sent(s, c):
        piece(s).wait_send()
        spread_piece(s).wait_send()
        return c

    lax.fori_loop(1, 16, wait_sent, 0)
    for s in range(1, 4):
        near(s).wait_send()

    @pl.when(p == 0)
    def _():
        for n in range(6):
            far(n, *to_left[n]).wait_send()

    @pl.when(p == 3)
    def _():
        for n in range(6):
            far(n, *to_right[n]).wait_send()

    swap.wait_recv()
    scale = 1.0 / math.sqrt(4 * 64 * 512)
    for h in range(2):
        d1_ref[:, h * 128 : h * 128 + 128] = fin[h, 0:768].astype(F32) * scale
        d2_ref[:, h * 128 : h * 128 + 128] = fin[h, 768:1536].astype(F32) * scale
    swap.wait_send()


def body(state_field, first_weight, second_weight, quadrature, lat_offsets, lon_offsets, cotangent):
    def turned(field):
        return jnp.transpose(field[0], (1, 2, 0)).reshape(256, 256)

    def back(field):
        return jnp.transpose(field.reshape(2, 128, 256), (2, 0, 1))[None]

    vmem = pl.BlockSpec(memory_space=pltpu.VMEM)
    dma = pltpu.SemaphoreType.DMA
    lo, sg, d1, d2 = pl.pallas_call(
        kernel,
        out_shape=(
            jax.ShapeDtypeStruct((256, 256), BF),
            jax.ShapeDtypeStruct((256, 256), BF),
            jax.ShapeDtypeStruct((768, 256), F32),
            jax.ShapeDtypeStruct((768, 256), F32),
        ),
        in_specs=[vmem] * 7,
        out_specs=[vmem] * 4,
        scratch_shapes=[
            pltpu.VMEM((2, 5, 4, 32, 256), BF),
            pltpu.VMEM((2, 5, 4, 32, 256), BF),
            pltpu.VMEM((2, 8, 128), F32),
            pltpu.VMEM((2, 8, 128), F32),
            pltpu.VMEM((2, 384, 512), BF),
            pltpu.VMEM((2, 384, 512), BF),
            pltpu.VMEM((3, 256, 256), BF),
            pltpu.VMEM((3, 256, 256), BF),
            pltpu.VMEM((256, 256), F32),
            pltpu.VMEM((2, 1536, 128), BF),
            pltpu.VMEM((1536, 128), BF),
            pltpu.VMEM((1536, 128), BF),
            pltpu.VMEM((15, PIECE, 128), BF),
            pltpu.VMEM((4, PIECE, 128), BF),
            pltpu.VMEM((4, PIECE, 128), BF),
            pltpu.VMEM((2, 1536, 128), BF),
            dma((12,)), dma((12,)),
            dma((10,)), dma((10,)),
            dma((2,)), dma((2,)),
            dma((15,)), dma((15,)),
            dma((3,)), dma((4,)),
            dma((6,)), dma((4,)),
            dma((15,)), dma((15,)),
            dma((1,)), dma((1,)),
        ],
        compiler_params=pltpu.CompilerParams(collective_id=0, has_side_effects=True, vmem_limit_bytes=48 * 2**20),
        cost_estimate=pl.CostEstimate(flops=1_500_000_000, bytes_accessed=4_000_000, transcendentals=65536),
        name="conv_pair",
    )(turned(state_field), turned(cotangent), first_weight, second_weight, quadrature, lat_offsets, lon_offsets)
    return back(lo), back(sg), d1.reshape(3, 256, 256), d2.reshape(3, 256, 256)


def solution(mesh):
    in_specs = (
        P("ens", None, "lat", "lon"),
        P(),
        P(),
        P("lat", None, None),
        P("lat", None, None),
        P("lat", None, None),
        P("ens", None, "lat", "lon"),
    )
    out_specs = (P("ens", None, "lat", "lon"), P("ens", None, "lat", "lon"), P(), P())
    return jax.shard_map(body, mesh=mesh, in_specs=in_specs, out_specs=out_specs, check_vma=False)
```

time: 625 us -> 68.3 us (0.11)
  waiting for transfers between devices: 484 us -> 0 us
  Pallas kernels: 0 us -> 58.9 us
  local copies, waits for them, and re-layouts: 66.4 us -> 8.38 us
  starting transfers between devices: 46.5 us -> 0 us
  between operations: 14.7 us -> 0.69 us
  matrix products: 6.82 us -> 0 us
    psum x1 -> x0, waiting for transfers between devices: 478 us -> none  [body(): lax.psum((first_sum, second_sum), ('ens', 'lat', 'lon'))]
    pallas_call x0 -> x1, Pallas kernels: none -> 58.9 us  [body(): pl.pallas_call(kernel, out_shape=(jax.ShapeDtypeStruct((256, 256), BF), j...]
    scatter-add x4 -> x0, local copies, waits for them, and re-layouts: 56.9 us -> none  [the longest x1 42.8 us: carry_back(): core_block.at[:, :, col_count - LON_REACH:].add(lon_pass(left_rim, -1))]
    ppermute x16 -> x0, starting transfers between devices: 46.5 us -> none  [the longest x4 12.7 us: passed_along_2(): lax.ppermute(value, axis, [(source, source + steps) for source in range(l...]
    dot_general x12 -> x0, matrix products: 6.82 us -> none  [the longest x2 2.37 us: filter_term(): jnp.einsum('oij,cikj->koc', gradient, spreaded, preferred_element_type=jn...]
  transfers between devices with their start and end apart: 17 -> 0, of which waited for: 4 -> 0; matrix products, arithmetic and copies ran while one was open for 11% -> 0% of each run, Pallas kernels for 0% -> 0%
where the time goes in v1:
time: 68.3 us; the launch traced here: 68 us
  Pallas kernels  58.9 us (86%)
  local copies, waits for them, and re-layouts  8.38 us (12%)
  between operations  0.69 us (1%)
    pallas_call x1, Pallas kernels, body(): pl.pallas_call(kernel, out_shape=(jax.ShapeDtypeStruct((256, 256), BF), j...  58.9 us
    unnamed x11, local copies, waits for them, and re-layouts  4.79 us
    transpose x2, local copies, waits for them, and re-layouts, turned(): return jnp.transpose(field[0], (1, 2, 0)).reshape(256, 256)  2.03 us
    reshape x2, local copies, waits for them, and re-layouts, back(): return jnp.transpose(field.reshape(2, 128, 256), (2, 0, 1))[None]  1.56 us

profile of v1, /device:TPU:1, one launch (start us, length us, event | category | flops | bytes accessed | tf_op | source)
XLA Modules:
  0.0 68.0 jit_solution(18409939394516188031)
XLA Ops:
  0.6 0.0 copy-start.2
  0.6 0.0 copy-start
  0.7 0.7 copy-done.2
  1.3 0.7 %copy.14.lato_ref = s32[2,3,12]{2,1,0:T(4,128)S(1)} copy(s32[2,3,12]{2,0,1:T(2,128)} %param.11) | data formatting | bytes 576 | tf_op args[4]
  2.0 0.7 %copy.15.lono_ref = s32[2,3,12]{2,1,0:T(4,128)S(1)} copy(s32[2,3,12]{2,0,1:T(2,128)} %param.12) | data formatting | bytes 576 | tf_op args[5]
  2.7 1.0 %copy.11 = bf16[2,128,256]{2,1,0:T(8,128)(2,1)S(1)} copy(bf16[2,128,256]{1,0,2:T(2,128)(2,1)} %bitcast.24) | data formatting | bytes 262144 | tf_op jit(solution)/shard_map/transpose | solution.py:348
  3.7 1.0 %copy.12 = bf16[2,128,256]{2,1,0:T(8,128)(2,1)S(1)} copy(bf16[2,128,256]{1,0,2:T(2,128)(2,1)} %bitcast.25) | data formatting | bytes 262144 | tf_op jit(solution)/shard_map/transpose | solution.py:348
  4.7 0.0 copy-done
  4.7 0.0 copy-start.1
  4.8 1.0 %copy-done.1 = bf16[3,256,256]{2,1,0:T(8,128)(2,1)S(1)} copy-done((bf16[3,256,256]{2,1,0:T(8,128)(2,1)S(1)}, bf16[3,256,256]{2,1,0:T(8,128)(2,1)}, u32[]{:S(2)}) %copy-start.1) | copy-done | bytes 393240
  5.7 58.9 %conv_pair.1 = (bf16[256,256]{1,0:T(8,128)(2,1)S(1)}, bf16[256,256]{1,0:T(8,128)(2,1)S(1)}, f32[768,256]{1,0:T(8,128)S(1)}, f32[768,256]{1,0:T(8,128)S(1)}) custom-call(bf16[256,256]{1,0:T(8,128)(2,1)S(1)} %bitcast.22, bf16[256,256]{1,0:T(8,128)(2,1)S(1)} %bitcast.23, bf16[3,256,256]{2,1,0:T(8,128)(2,1)S(1)} %copy-done, bf16[3,256,256]{2,1,0:T(8,128)(2,1)S(1)} %copy-done.1, ...), custom_call_target="tpu_custom_call" | custom-call | flops 1500000000 | bytes 4000000 | tf_op jit(solution)/shard_map/conv_pair/pallas_call | solution.py:355
  64.7 0.8 %copy.16 = bf16[2,128,256]{1,0,2:T(2,128)(2,1)} copy(bf16[2,128,256]{2,1,0:T(8,128)(2,1)S(1)} %bitcast.21) | data formatting | bytes 262144 | tf_op jit(solution)/shard_map/reshape | solution.py:351
  65.5 0.8 %copy.17 = bf16[2,128,256]{1,0,2:T(2,128)(2,1)} copy(bf16[2,128,256]{2,1,0:T(8,128)(2,1)S(1)} %bitcast.20) | data formatting | bytes 262144 | tf_op jit(solution)/shard_map/reshape | solution.py:351
  66.2 0.9 %copy.20 = f32[3,256,256]{2,1,0:T(8,128)} copy(f32[3,256,256]{2,1,0:T(8,128)S(1)} %bitcast.19) | data formatting | bytes 1572864
  67.1 0.9 %copy.21 = f32[3,256,256]{2,1,0:T(8,128)} copy(f32[3,256,256]{2,1,0:T(8,128)S(1)} %bitcast.18) | data formatting | bytes 1572864
  (1 shorter events, 0.0 us)
Async XLA Ops:
  0.6 0.7 %copy-start.2 = (f32[2,3,12]{2,0,1:T(2,128)S(1)}, f32[2,3,12]{2,0,1:T(2,128)}, u32[]{:S(2)}) copy-start(f32[2,3,12]{2,0,1:T(2,128)} %param.10) | copy-start | bytes 868
  0.6 4.1 %copy-start = (bf16[3,256,256]{2,1,0:T(8,128)(2,1)S(1)}, bf16[3,256,256]{2,1,0:T(8,128)(2,1)}, u32[]{:S(2)}) copy-start(bf16[3,256,256]{2,1,0:T(8,128)(2,1)} %w1_ref.1) | copy-start | bytes 1179652
  4.7 1.0 %copy-start.1 = (bf16[3,256,256]{2,1,0:T(8,128)(2,1)S(1)}, bf16[3,256,256]{2,1,0:T(8,128)(2,1)}, u32[]{:S(2)}) copy-start(bf16[3,256,256]{2,1,0:T(8,128)(2,1)} %w2_ref.1) | copy-start | bytes 1179652

commit v2 on v1

v2 whole, which is shorter than its diff:
```python
import math

import jax
import jax.numpy as jnp
from jax import lax
from jax.experimental import pallas as pl
from jax.experimental.pallas import tpu as pltpu
from jax.sharding import PartitionSpec as P

MESH = pl.DeviceIdType.MESH
BF = jnp.bfloat16
F32 = jnp.float32

PIECE = 48


def dot(a, b, ca, cb):
    return lax.dot_general(a, b, (((ca,), (cb,)), ((), ())), preferred_element_type=F32)


def copy_to(src, dst, send, recv, device):
    return pltpu.make_async_remote_copy(
        src_ref=src, dst_ref=dst, send_sem=send, recv_sem=recv, device_id=device, device_id_type=MESH
    )


def tap_rows(quad, lat_off, lon_off, a, sign):
    lane = lax.broadcasted_iota(jnp.int32, (3, 128), 1)
    offset = jnp.where(lane < 64, lane, lane - 128) * sign
    total = jnp.zeros((3, 128), F32)
    for s in range(12):
        hit = (lon_off[:, s : s + 1] == offset) & (lat_off[:, s : s + 1] == a - 1)
        total = total + jnp.where(hit, quad[:, s : s + 1], 0.0)
    return total.astype(BF).astype(F32)


def banded(row, count, first, shift):
    wide = jnp.broadcast_to(row, (count, 128))
    return pltpu.roll(wide, (shift + first) % 128, 1, stride=1, stride_axis=0)


def main_band(row):
    block = banded(row, 128, 0, 0)
    gap = lax.broadcasted_iota(jnp.int32, (128, 128), 1) - lax.broadcasted_iota(jnp.int32, (128, 128), 0)
    return jnp.where((gap <= 4) & (gap >= -4), block, 0.0).astype(BF)


def edge_band(rows_of, first):
    total = jnp.zeros((16, 128), F32)
    lane = lax.broadcasted_iota(jnp.int32, (16, 128), 1)
    cell = lax.broadcasted_iota(jnp.int32, (16, 128), 0) + first
    for place, row in rows_of:
        t = lane - 32 * place
        block = banded(row, 16, first, 32 * place + 16)
        gap = jnp.where(t < 16, t - 16, t + 112) - cell
        ok = (t >= 0) & (t < 32) & (gap <= 4) & (gap >= -4)
        total = total + jnp.where(ok, block, 0.0)
    return total.astype(BF)


def kernel(
    x_hbm, g_hbm, w1_hbm, w2_hbm, quad_hbm, lato_hbm, lono_hbm,
    lo_hbm, sg_hbm, fin_hbm,
    lo_ref, sg_ref, fin, xg, w1_ref, w2_ref, quad_ref, lato_ref, lono_ref, sel,
    ext1, ext2, bsend, brecv, bandf, banda, u_ref, t_ref, slope,
    gs, crecv, xs, xrecv, zrecv, zgroup,
    si, s1, r1, s2, r2, sc, rc, sx, rx, sz, rz, sf, rf, sa, ra, sd, rd, so, tok,
):
    e, l, x = lax.axis_index("ens"), lax.axis_index("lat"), lax.axis_index("lon")
    yh, core = e // 2, e % 2
    z, yl = l // 2, l % 2
    y = yh * 2 + yl
    me = y * 4 + x
    p, grp = z % 4, z // 4
    up, down = (l + 31) % 32, (l + 1) % 32
    left, right = (x + 3) % 4, (x + 1) % 4
    partner = (yh * 2 + 1 - core, l, x)
    across = ((1 - yh) * 2 + core, z * 2 + 1 - yl, x)

    def xy_peer(s):
        xx, yy = (x + s % 4) % 4, (y + s // 4) % 4
        return yy * 4 + xx, ((yy // 2) * 2 + core, z * 2 + yy % 2, xx)

    def z_device(zz):
        return (e, zz * 2 + yl, x)

    barrier = pltpu.get_barrier_semaphore()

    def signal(sem, device):
        pl.semaphore_signal(sem, inc=1, device_id=device, device_id_type=MESH)

    for ll, xx in ((up, x), (down, x), (l, left), (l, right), (up, left), (up, right), (down, left), (down, right)):
        signal(barrier, (e, ll, xx))
    signal(barrier, partner)
    signal(barrier, across)

    loads = [
        pltpu.make_async_copy(src, dst, si.at[n])
        for n, (src, dst) in enumerate(
            (
                (x_hbm, xg.at[0]), (quad_hbm, quad_ref), (lato_hbm, lato_ref), (lono_hbm, lono_ref),
                (g_hbm, xg.at[1]), (w1_hbm, w1_ref), (w2_hbm, w2_ref),
            )
        )
    ]
    for c in loads:
        c.start()

    for r in range(2):
        at = lax.broadcasted_iota(jnp.int32, (512, 256), 0)
        want = 2 * lax.broadcasted_iota(jnp.int32, (512, 256), 1) + r
        sel[r] = jnp.where(at == want, 1.0, 0.0).astype(BF)

    def turn(f):
        for r in range(2):
            ext1[f, 1 + r] = dot(xg[f], sel[r], 0, 0).astype(BF).reshape(4, 32, 256)

    loads[0].wait()
    turn(0)
    for n in (1, 2, 3):
        loads[n].wait()
    taps = [(quad_ref[:, i], lato_ref[:, i], lono_ref[:, i]) for i in range(2)]
    adj = [[tap_rows(*taps[i], a, -1) for a in range(3)] for i in range(2)]
    bsend[...] = jnp.zeros((2, 8, 128), F32)
    bsend[0, 0:3] = adj[0][0]
    bsend[1, 0:3] = adj[1][2]
    loads[4].wait()
    turn(1)

    pl.semaphore_wait(barrier, 10)

    first = [
        copy_to(bsend.at[0], brecv.at[1], s1.at[0], r1.at[0], (e, up, x)),
        copy_to(bsend.at[1], brecv.at[0], s1.at[1], r1.at[1], (e, down, x)),
        copy_to(ext1.at[0, 1], ext1.at[0, 4], s1.at[2], r1.at[2], (e, up, x)),
        copy_to(ext1.at[0, 2], ext1.at[0, 0], s1.at[3], r1.at[3], (e, down, x)),
    ]

    def edges(ext, s, r, n):
        return [
            copy_to(ext.at[:, 1:3, 3, 16:32], ext.at[:, 3, 1:3, 0:16], s.at[n], r.at[n], (e, l, right)),
            copy_to(ext.at[:, 1:3, 0, 0:16], ext.at[:, 3, 1:3, 16:32], s.at[n + 1], r.at[n + 1], (e, l, left)),
            copy_to(ext.at[:, 2, 3, 16:32], ext.at[:, 3, 0, 0:16], s.at[n + 2], r.at[n + 2], (e, down, right)),
            copy_to(ext.at[:, 2, 0, 0:16], ext.at[:, 3, 0, 16:32], s.at[n + 3], r.at[n + 3], (e, down, left)),
            copy_to(ext.at[:, 1, 3, 16:32], ext.at[:, 3, 3, 0:16], s.at[n + 4], r.at[n + 4], (e, up, right)),
            copy_to(ext.at[:, 1, 0, 0:16], ext.at[:, 3, 3, 16:32], s.at[n + 5], r.at[n + 5], (e, up, left)),
        ]

    first += edges(ext1, s1, r1, 6)
    first += [
        copy_to(ext1.at[1, 1], ext1.at[1, 4], s1.at[4], r1.at[4], (e, up, x)),
        copy_to(ext1.at[1, 2], ext1.at[1, 0], s1.at[5], r1.at[5], (e, down, x)),
    ]
    for c in first:
        c.start()
    for device in ((e, up, x), (e, down, x), (e, l, left), (e, l, right), across):
        signal(tok.at[0], device)

    top, bottom = (l > 0).astype(F32), (l < 31).astype(F32)
    col = ((0, 1, 2, 3), (0, 1, 3, 2))

    def put_bands(band, i, rows):
        for k in range(3):
            out = slice(k * 128, k * 128 + 128)
            for n in range(3):
                c = col[i][n] * 128
                band[i, out, c : c + 128] = main_band(rows[n][k : k + 1])
            c = col[i][3] * 128
            places = [(i + n, rows[n][k : k + 1]) for n in range(3)]
            band[i, k * 128 : k * 128 + 16, c : c + 128] = edge_band(places, 0)
            band[i, k * 128 + 16 : k * 128 + 112, c : c + 128] = jnp.zeros((96, 128), BF)
            band[i, k * 128 + 112 : k * 128 + 128, c : c + 128] = edge_band(places, 112)

    fwd = [[tap_rows(*taps[i], a, 1) for a in range(3)] for i in range(2)]
    put_bands(bandf, 0, [fwd[0][0] * top, fwd[0][1], fwd[0][2]])
    put_bands(bandf, 1, [fwd[1][0], fwd[1][1], fwd[1][2] * bottom])
    pl.semaphore_wait(tok.at[0], 5)
    two = (e, l, (x + 2) % 4), ((1 - yh) * 2 + core, l, x), z_device((z + 1) % 16), z_device((z + 15) % 16)
    for device in two:
        signal(tok.at[1], device)
    first[0].wait_recv()
    first[1].wait_recv()
    put_bands(banda, 0, [brecv[0, 0:3] * top, adj[0][1], adj[1][0]])
    put_bands(banda, 1, [adj[0][2], adj[1][1], brecv[1, 0:3] * bottom])

    def spread(band, ext, f, out):
        for i in range(2):
            cells = ext[f, i : i + 4].reshape(512, 256)
            got = dot(band[i], cells, 1, 0).astype(BF)
            for k in range(3):
                out[k, i * 128 : i * 128 + 128] = got[k * 128 : k * 128 + 128]

    def mixed(spreaded, weight, cw):
        total = dot(spreaded[0], weight[0], 1, cw)
        for k in range(1, 3):
            total = total + dot(spreaded[k], weight[k], 1, cw)
        return total

    loads[5].wait()
    loads[6].wait()
    for c in first[2:10]:
        c.wait_recv()
    spread(bandf, ext1, 0, u_ref)
    hidden = mixed(u_ref, w1_ref, 1)
    root = math.sqrt(2.0 / math.pi)
    square = hidden * hidden
    bend = jnp.tanh(root * hidden * (1.0 + 0.044715 * square))
    act = (0.5 * hidden * (1.0 + bend)).astype(BF)
    slope[...] = 0.5 * (1.0 + bend) + (0.5 * root) * hidden * (1.0 - bend * bend) * (1.0 + (3 * 0.044715) * square)
    ext2[0, 1:3] = act.reshape(2, 4, 32, 256)

    first[10].wait_recv()
    first[11].wait_recv()
    spread(banda, ext1, 1, t_ref)

    def put_grad(ch, row, value):
        value = value.astype(BF)
        gs[ch, 0, row : row + 256] = value[:, :128]
        gs[ch, 1, row : row + 256] = value[:, 128:]

    cores = [
        copy_to(gs.at[ch, 1 - core], crecv.at[ch], sc.at[ch], rc.at[ch], partner) for ch in range(2)
    ]
    for k in range(3):
        put_grad(0, k * 256, dot(t_ref[k], act, 0, 0))
    cores[0].start()
    act_grad = mixed(t_ref, w2_ref, 0).astype(BF).astype(F32)
    hid_grad = (act_grad * slope[...]).astype(BF)
    ext2[1, 1:3] = hid_grad.reshape(2, 4, 32, 256)
    for k in range(3):
        put_grad(1, k * 256, dot(hid_grad, u_ref[k], 0, 0))
    cores[1].start()
    pl.semaphore_wait(tok.at[1], 4)
    for d in (2, 14):
        signal(tok.at[2], z_device((z + d) % 16))

    def piece(ch, s):
        peer, device = xy_peer(s)
        rows = pl.ds(pl.multiple_of(peer * PIECE, 16), PIECE)
        return copy_to(xs.at[ch, rows], xrecv.at[ch, s - 1], sx.at[ch, s - 1], rx.at[ch, s - 1], device)

    for ch in range(2):
        cores[ch].wait_recv()
        xs[ch] = (gs[ch, core].astype(F32) + crecv[ch].astype(F32)).astype(BF)

        def send_piece(s, c, ch=ch):
            piece(ch, s).start()
            return c

        lax.fori_loop(1, 16, send_piece, 0)

    pl.semaphore_wait(tok.at[2], 2)
    for d in (4, 12):
        signal(tok.at[3], z_device((z + d) % 16))

    mine = pl.ds(pl.multiple_of(me * PIECE, 16), PIECE)

    def near(ch, s):
        return copy_to(zrecv.at[ch, p], zrecv.at[ch, p], sz.at[ch, s - 1], rz.at[ch, p], z_device(grp * 4 + (p + s) % 4))

    def near_in(ch, s):
        q = (p + s) % 4
        return copy_to(zrecv.at[ch, q], zrecv.at[ch, q], sz.at[ch, s - 1], rz.at[ch, q], z_device(grp * 4 + q))

    for ch in range(2):

        def add_piece(s, total, ch=ch):
            piece(ch, s).wait_recv()
            return total + xrecv[ch, s - 1].astype(F32)

        zrecv[ch, p] = lax.fori_loop(1, 16, add_piece, xs[ch, mine].astype(F32)).astype(BF)
        for s in range(1, 4):
            near(ch, s).start()

    second = [
        copy_to(ext2.at[:, 1], ext2.at[:, 4], s2.at[0], r2.at[0], (e, up, x)),
        copy_to(ext2.at[:, 2], ext2.at[:, 0], s2.at[1], r2.at[1], (e, down, x)),
    ]
    second += edges(ext2, s2, r2, 2)
    for c in second:
        c.start()

    def far(ch, n, group, member):
        return copy_to(
            zgroup.at[ch, grp], zgroup.at[ch, grp], sf.at[ch, n], rf.at[ch, grp], z_device(group * 4 + member)
        )

    before, after, opposite = (grp + 3) % 4, (grp + 1) % 4, (grp + 2) % 4
    to_left = [(opposite, 2), (opposite, 3), (before, 0), (before, 1), (before, 2), (before, 3)]
    to_right = [(opposite, 1), (opposite, 0), (after, 3), (after, 2), (after, 1), (after, 0)]

    def all_four(ref):
        total = ref[0].astype(F32)
        for q in range(1, 4):
            total = total + ref[q].astype(F32)
        return total.astype(BF)

    pl.semaphore_wait(tok.at[3], 2)
    for ch in range(2):
        for s in range(1, 4):
            near_in(ch, s).wait_recv()
        zgroup[ch, grp] = all_four(zrecv.at[ch])

        @pl.when(p == 0)
        def _(ch=ch):
            for n in range(6):
                far(ch, n, *to_left[n]).start()

        @pl.when(p == 3)
        def _(ch=ch):
            for n in range(6):
                far(ch, n, *to_right[n]).start()

    def spread_piece(ch, s):
        cells = fin.at[ch, core, mine]
        return copy_to(cells, cells, sa.at[ch, s - 1], ra.at[ch, s - 1], xy_peer(s)[1])

    for ch in range(2):
        for s in range(1, 4):
            q = (grp + s) % 4
            cells = zgroup.at[ch, q]
            copy_to(cells, cells, sf.at[ch, 0], rf.at[ch, q], z_device(q * 4)).wait_recv()
        fin[ch, core, mine] = all_four(zgroup.at[ch])

        def send_back(s, c, ch=ch):
            spread_piece(ch, s).start()
            return c

        lax.fori_loop(1, 16, send_back, 0)

    def turned_back(cells):
        return (dot(sel[0], cells[0:128], 1, 1) + dot(sel[1], cells[128:256], 1, 1)).astype(BF)

    for c in second:
        c.wait_recv()
    spread(bandf, ext2, 0, u_ref)
    lo_ref[...] = turned_back(mixed(u_ref, w2_ref, 1).astype(BF))
    spread(banda, ext2, 1, t_ref)
    sg_ref[...] = turned_back(mixed(t_ref, w1_ref, 0).astype(BF))
    stores = [
        pltpu.make_async_copy(lo_ref, lo_hbm, so.at[0]),
        pltpu.make_async_copy(sg_ref, sg_hbm, so.at[1]),
        pltpu.make_async_copy(fin.at[0], fin_hbm.at[0], so.at[2]),
        pltpu.make_async_copy(fin.at[1], fin_hbm.at[1], so.at[3]),
    ]
    stores[0].start()
    stores[1].start()

    for c in first + second + cores:
        c.wait_send()
    for ch in range(2):

        def wait_sent(s, c, ch=ch):
            piece(ch, s).wait_send()
            return c

        lax.fori_loop(1, 16, wait_sent, 0)
        for s in range(1, 4):
            near(ch, s).wait_send()

        @pl.when(p == 0)
        def _(ch=ch):
            for n in range(6):
                far(ch, n, *to_left[n]).wait_send()

        @pl.when(p == 3)
        def _(ch=ch):
            for n in range(6):
                far(ch, n, *to_right[n]).wait_send()

    swaps = [copy_to(fin.at[ch, core], fin.at[ch, core], sd.at[ch], rd.at[ch], partner) for ch in range(2)]
    for ch in range(2):

        def wait_back(s, c, ch=ch):
            spread_piece(ch, s).wait()
            return c

        lax.fori_loop(1, 16, wait_back, 0)
        swaps[ch].start()
    for ch in range(2):
        swaps[ch].wait()
        stores[2 + ch].start()
    for c in stores:
        c.wait()


def finish(lo_in, sg_in, fin_in, lo_hbm, sg_hbm, d1_hbm, d2_hbm, cells, fin, d_ref, sems):
    pieces = [(n, k) for n in range(2) for k in range(3)]
    loads, stores = [], []
    for n, k in pieces:
        rows = slice(k * 256, k * 256 + 256)
        loads.append(pltpu.make_async_copy(fin_in.at[n, :, rows], fin.at[n, k], sems.at[3 * n + k]))
        loads[-1].start()
    for n, (src, dst) in enumerate(((lo_in, lo_hbm), (sg_in, sg_hbm))):
        loads.append(pltpu.make_async_copy(src, cells.at[n], sems.at[6 + n]))
        loads[-1].start()
        stores.append(pltpu.make_async_copy(cells.at[n], dst, sems.at[14 + n]))
    scale = 1.0 / math.sqrt(4 * 64 * 512)
    for (n, k), load in zip(pieces, loads):
        load.wait()
        for h in range(2):
            d_ref[n, k, :, h * 128 : h * 128 + 128] = fin[n, k, h].astype(F32) * scale
        stores.append(pltpu.make_async_copy(d_ref.at[n, k], (d2_hbm, d1_hbm)[n].at[k], sems.at[8 + 3 * n + k]))
        stores[-1].start()
    for n in range(2):
        loads[6 + n].wait()
        stores[n].start()
    for c in stores:
        c.wait()


def body(state_field, first_weight, second_weight, quadrature, lat_offsets, lon_offsets, cotangent):
    anywhere = pl.BlockSpec(memory_space=pl.ANY)
    dma = pltpu.SemaphoreType.DMA
    lo, sg, fin = pl.pallas_call(
        kernel,
        out_shape=(
            jax.ShapeDtypeStruct((512, 128), BF),
            jax.ShapeDtypeStruct((512, 128), BF),
            jax.ShapeDtypeStruct((2, 2, 768, 128), BF),
        ),
        in_specs=[anywhere] * 7,
        out_specs=[anywhere] * 3,
        scratch_shapes=[
            pltpu.VMEM((512, 128), BF),
            pltpu.VMEM((512, 128), BF),
            pltpu.VMEM((2, 2, 768, 128), BF),
            pltpu.VMEM((2, 512, 128), BF),
            pltpu.VMEM((3, 256, 256), BF),
            pltpu.VMEM((3, 256, 256), BF),
            pltpu.VMEM((3, 2, 12), F32),
            pltpu.VMEM((3, 2, 12), jnp.int32),
            pltpu.VMEM((3, 2, 12), jnp.int32),
            pltpu.VMEM((2, 512, 256), BF),
            pltpu.VMEM((2, 5, 4, 32, 256), BF),
            pltpu.VMEM((2, 5, 4, 32, 256), BF),
            pltpu.VMEM((2, 8, 128), F32),
            pltpu.VMEM((2, 8, 128), F32),
            pltpu.VMEM((2, 384, 512), BF),
            pltpu.VMEM((2, 384, 512), BF),
            pltpu.VMEM((3, 256, 256), BF),
            pltpu.VMEM((3, 256, 256), BF),
            pltpu.VMEM((256, 256), F32),
            pltpu.VMEM((2, 2, 768, 128), BF),
            pltpu.VMEM((2, 768, 128), BF),
            pltpu.VMEM((2, 768, 128), BF),
            pltpu.VMEM((2, 15, PIECE, 128), BF),
            pltpu.VMEM((2, 4, PIECE, 128), BF),
            pltpu.VMEM((2, 4, PIECE, 128), BF),
            dma((7,)),
            dma((12,)), dma((12,)),
            dma((8,)), dma((8,)),
            dma((2,)), dma((2,)),
            dma((2, 15)), dma((2, 15)),
            dma((2, 3)), dma((2, 4)),
            dma((2, 6)), dma((2, 4)),
            dma((2, 15)), dma((2, 15)),
            dma((2,)), dma((2,)),
            dma((4,)),
            pltpu.SemaphoreType.REGULAR((4,)),
        ],
        compiler_params=pltpu.CompilerParams(collective_id=0, has_side_effects=True, vmem_limit_bytes=60 * 2**20),
        cost_estimate=pl.CostEstimate(flops=1_500_000_000, bytes_accessed=4_000_000, transcendentals=65536),
        name="conv_pair",
    )(
        state_field.reshape(512, 128),
        cotangent.reshape(512, 128),
        first_weight,
        second_weight,
        *(jnp.transpose(t, (1, 0, 2)) for t in (quadrature, lat_offsets, lon_offsets)),
    )
    lo, sg, d1, d2 = pl.pallas_call(
        finish,
        out_shape=(
            jax.ShapeDtypeStruct((512, 128), BF),
            jax.ShapeDtypeStruct((512, 128), BF),
            jax.ShapeDtypeStruct((3, 256, 256), F32),
            jax.ShapeDtypeStruct((3, 256, 256), F32),
        ),
        in_specs=[anywhere] * 3,
        out_specs=[anywhere] * 4,
        scratch_shapes=[
            pltpu.VMEM((2, 512, 128), BF),
            pltpu.VMEM((2, 3, 2, 256, 128), BF),
            pltpu.VMEM((2, 3, 256, 256), F32),
            dma((16,)),
        ],
        compiler_params=pltpu.CompilerParams(vmem_limit_bytes=60 * 2**20),
        name="put_out",
    )(lo, sg, fin)
    return lo.reshape(1, 256, 2, 128), sg.reshape(1, 256, 2, 128), d1, d2


def solution(mesh):
    in_specs = (
        P("ens", None, "lat", "lon"),
        P(),
        P(),
        P("lat", None, None),
        P("lat", None, None),
        P("lat", None, None),
        P("ens", None, "lat", "lon"),
    )
    out_specs = (P("ens", None, "lat", "lon"), P("ens", None, "lat", "lon"), P(), P())
    return jax.shard_map(body, mesh=mesh, in_specs=in_specs, out_specs=out_specs, check_vma=False)
```

time: 68.3 us -> 58 us (0.85)
  local copies, waits for them, and re-layouts: 8.38 us -> 0 us
  Pallas kernels: 58.9 us -> 57.2 us
    unnamed x11 -> x0, local copies, waits for them, and re-layouts: 4.79 us -> none
    transpose x2 -> x0, local copies, waits for them, and re-layouts: 2.03 us -> none  [turned(): return jnp.transpose(field[0], (1, 2, 0)).reshape(256, 256)]
    pallas_call x1 -> x2, Pallas kernels: 58.9 us -> 57.2 us  [the longest x1 54.9 us: body(): pl.pallas_call(kernel, out_shape=(jax.ShapeDtypeStruct((512, 128), BF), j...]
    reshape x2 -> x0, local copies, waits for them, and re-layouts: 1.56 us -> none  [back(): return jnp.transpose(field.reshape(2, 128, 256), (2, 0, 1))[None]]
where the time goes in v2:
time: 58 us; the launch traced here: 57.8 us
  Pallas kernels  57.2 us (99%)
  between operations  0.64 us (1%)
    pallas_call x1, Pallas kernels, body(): pl.pallas_call(kernel, out_shape=(jax.ShapeDtypeStruct((512, 128), BF), j...  54.9 us
    pallas_call x1, Pallas kernels, body(): pl.pallas_call(finish, out_shape=(jax.ShapeDtypeStruct((512, 128), BF), j...  2.29 us

profile of v2, /device:TPU:1, one launch (start us, length us, event | category | flops | bytes accessed | tf_op | source)
XLA Modules:
  0.0 57.8 jit_solution(16266924552146646350)
XLA Ops:
  0.6 54.9 %conv_pair.1 = (bf16[512,128]{1,0:T(8,128)(2,1)}, bf16[512,128]{1,0:T(8,128)(2,1)}, bf16[2,2,768,128]{3,2,1,0:T(8,128)(2,1)}) custom-call(bf16[512,128]{1,0:T(8,128)(2,1)} %bitcast.7, bf16[512,128]{1,0:T(8,128)(2,1)} %bitcast.8, bf16[3,256,256]{2,1,0:T(8,128)(2,1)} %w1_hbm.1, bf16[3,256,256]{2,1,0:T(8,128)(2,1)} %w2_hbm.1, f32[3,2,12]{2,1,0:T(2,128)} %bitcast.11, ...), custom_call_target="tpu_custom_call" | custom-call | flops 1500000000 | bytes 4000000 | tf_op jit(solution)/shard_map/conv_pair/pallas_call | solution.py:415
  55.5 2.3 %put_out.1 = (bf16[512,128]{1,0:T(8,128)(2,1)}, bf16[512,128]{1,0:T(8,128)(2,1)}, f32[3,256,256]{2,1,0:T(8,128)}, f32[3,256,256]{2,1,0:T(8,128)}) custom-call(bf16[512,128]{1,0:T(8,128)(2,1)} %get-tuple-element.11.lo_in, bf16[512,128]{1,0:T(8,128)(2,1)} %get-tuple-element.12.sg_in, bf16[2,2,768,128]{3,2,1,0:T(8,128)(2,1)} %get-tuple-element.13.fin_in), custom_call_target="tpu_custom_call" | custom-call | tf_op jit(solution)/shard_map/put_out/pallas_call | solution.py:472

commit v3 on v2

v3 whole, which is shorter than its diff:
```python
import math

import jax
import jax.numpy as jnp
from jax import lax
from jax.experimental import pallas as pl
from jax.experimental.pallas import tpu as pltpu
from jax.sharding import PartitionSpec as P

MESH = pl.DeviceIdType.MESH
BF = jnp.bfloat16
F32 = jnp.float32

PIECE = 48


def dot(a, b, ca, cb):
    return lax.dot_general(a, b, (((ca,), (cb,)), ((), ())), preferred_element_type=F32)


def copy_to(src, dst, send, recv, device):
    return pltpu.make_async_remote_copy(
        src_ref=src, dst_ref=dst, send_sem=send, recv_sem=recv, device_id=device, device_id_type=MESH
    )


def tap_rows(quad, lat_off, lon_off, sign):
    lane = lax.broadcasted_iota(jnp.int32, (8, 128), 1)
    code = 32 * (lat_off + 1) + sign * lon_off
    code = jnp.where(code < 0, code + 128, code)
    total = jnp.zeros((8, 128), F32)
    for s in range(12):
        total = total + jnp.where(lane == code[:, s : s + 1], quad[:, s : s + 1], 0.0)
    return total.astype(BF).astype(F32)


def one_tap(taps, a):
    lane = lax.broadcasted_iota(jnp.int32, (8, 128), 1)
    moved = taps if a == 0 else pltpu.roll(taps, 128 - 32 * a, 1)
    return jnp.where((lane < 5) | (lane > 123), moved, 0.0)


def banded(row, count, first, shift):
    wide = jnp.broadcast_to(row, (count, 128))
    return pltpu.roll(wide, (shift + first) % 128, 1, stride=1, stride_axis=0)


def put_main(band, i, out, c, row):
    block = banded(row, 128, 0, 0)
    lane = lax.broadcasted_iota(jnp.int32, (16, 128), 1)
    band[i, out : out + 16, c : c + 128] = jnp.where(lane < 64, block[0:16], 0.0).astype(BF)
    band[i, out + 16 : out + 112, c : c + 128] = block[16:112].astype(BF)
    band[i, out + 112 : out + 128, c : c + 128] = jnp.where(lane >= 64, block[112:128], 0.0).astype(BF)


def edge_band(rows_of, first):
    total = jnp.zeros((16, 128), F32)
    lane = lax.broadcasted_iota(jnp.int32, (16, 128), 1)
    for place, row in rows_of:
        t = lane - 32 * place
        block = banded(row, 16, first, 32 * place + 16)
        ok = (t >= 0) & (t < 16) if first == 0 else (t >= 16) & (t < 32)
        total = total + jnp.where(ok, block, 0.0)
    return total.astype(BF)


def kernel(
    x_hbm, g_hbm, w1_hbm, w2_hbm, quad_hbm, lato_hbm, lono_hbm,
    lo_ref, sg_ref, fin,
    xg, w1_ref, w2_ref, quad_ref, lato_ref, lono_ref, sel,
    ext1, ext2, bsend, brecv, bandf, banda, u_ref, t_ref, slope,
    gs, crecv, xs, xrecv, zrecv, zgroup,
    si, s1, r1, s2, r2, sc, rc, sx, rx, sz, rz, sf, rf, sa, ra, sd, rd, tok,
):
    e, l, x = lax.axis_index("ens"), lax.axis_index("lat"), lax.axis_index("lon")
    yh, core = e // 2, e % 2
    z, yl = l // 2, l % 2
    y = yh * 2 + yl
    me = y * 4 + x
    p, grp = z % 4, z // 4
    up, down = (l + 31) % 32, (l + 1) % 32
    left, right = (x + 3) % 4, (x + 1) % 4
    partner = (yh * 2 + 1 - core, l, x)
    across = ((1 - yh) * 2 + core, z * 2 + 1 - yl, x)

    def xy_peer(s):
        xx, yy = (x + s % 4) % 4, (y + s // 4) % 4
        return yy * 4 + xx, ((yy // 2) * 2 + core, z * 2 + yy % 2, xx)

    def far_first(n):
        def pick(i):
            return (2 + i + (i // 2) * (1 + 2 * (i % 2))) % 4

        return 4 * pick(n // 4) + pick(n % 4)

    def z_device(zz):
        return (e, zz * 2 + yl, x)

    loads = [
        pltpu.make_async_copy(src, dst, si.at[n])
        for n, (src, dst) in enumerate(
            (
                (x_hbm, xg.at[0]), (quad_hbm, quad_ref), (lato_hbm, lato_ref), (lono_hbm, lono_ref),
                (g_hbm, xg.at[1]), (w1_hbm, w1_ref), (w2_hbm, w2_ref),
            )
        )
    ]
    for c in loads:
        c.start()

    barrier = pltpu.get_barrier_semaphore()

    def signal(sem, device):
        pl.semaphore_signal(sem, inc=1, device_id=device, device_id_type=MESH)

    for ll, xx in ((up, x), (down, x), (l, left), (l, right), (up, left), (up, right), (down, left), (down, right)):
        signal(barrier, (e, ll, xx))
    signal(barrier, partner)
    signal(barrier, across)

    at = lax.broadcasted_iota(jnp.int32, (256, 256), 0)
    to = lax.broadcasted_iota(jnp.int32, (256, 256), 1)
    sel[...] = jnp.where(at == jnp.where(to < 128, 2 * to, 2 * to - 255), 1.0, 0.0).astype(BF)

    def turn(f):
        for h in range(2):
            got = dot(xg[f, h * 256 : h * 256 + 256], sel[...], 0, 0).astype(BF)
            for r in range(2):
                ext1[f, 1 + r, :, :, h * 128 : h * 128 + 128] = got[:, r * 128 : r * 128 + 128].reshape(4, 32, 128)

    def rows(ext, f, s, r, n):
        return [
            copy_to(ext.at[f, 1], ext.at[f, 4], s.at[n], r.at[n], (e, up, x)),
            copy_to(ext.at[f, 2], ext.at[f, 0], s.at[n + 1], r.at[n + 1], (e, down, x)),
        ]

    def edges(ext, f, s, r, n):
        return [
            copy_to(ext.at[f, 2, 3, 16:32], ext.at[f, 3, 0, 0:16], s.at[n], r.at[n], (e, down, right)),
            copy_to(ext.at[f, 2, 0, 0:16], ext.at[f, 3, 0, 16:32], s.at[n + 1], r.at[n + 1], (e, down, left)),
            copy_to(ext.at[f, 1, 3, 16:32], ext.at[f, 3, 3, 0:16], s.at[n + 2], r.at[n + 2], (e, up, right)),
            copy_to(ext.at[f, 1, 0, 0:16], ext.at[f, 3, 3, 16:32], s.at[n + 3], r.at[n + 3], (e, up, left)),
            copy_to(ext.at[f, 1:3, 3, 16:32], ext.at[f, 3, 1:3, 0:16], s.at[n + 4], r.at[n + 4], (e, l, right)),
            copy_to(ext.at[f, 1:3, 0, 0:16], ext.at[f, 3, 1:3, 16:32], s.at[n + 5], r.at[n + 5], (e, l, left)),
        ]

    first = [edges(ext1, f, s1, r1, 8 * f) + rows(ext1, f, s1, r1, 8 * f + 6) for f in range(2)]
    first.append(
        [
            copy_to(bsend, brecv.at[1], s1.at[16], r1.at[16], (e, up, x)),
            copy_to(bsend, brecv.at[0], s1.at[17], r1.at[17], (e, down, x)),
        ]
    )
    loads[0].wait()
    turn(0)
    pl.semaphore_wait(barrier, 10)
    for c in first[0]:
        c.start()
    loads[4].wait()
    turn(1)
    for c in first[1]:
        c.start()
    for n in (1, 2, 3):
        loads[n].wait()
    pad = jnp.zeros((2, 12), jnp.int32)
    lato = jnp.concatenate([lato_ref[:, 0], lato_ref[:, 1], pad])
    lono = jnp.concatenate([lono_ref[:, 0], lono_ref[:, 1], pad])
    quad = jnp.concatenate([quad_ref[:, 0], quad_ref[:, 1], pad.astype(F32)])
    adjoint = tap_rows(quad, lato, lono, -1)
    bsend[...] = adjoint
    for c in first[2]:
        c.start()
    for device in ((e, up, x), (e, down, x), (e, l, left), (e, l, right), across):
        signal(tok.at[0], device)

    top, bottom = (l > 0).astype(F32), (l < 31).astype(F32)
    col = ((0, 1, 2, 3), (0, 1, 3, 2))

    def put_bands(band, i, rows):
        for k in range(3):
            for n in range(3):
                put_main(band, i, k * 128, col[i][n] * 128, rows[n](k))
            c = col[i][3] * 128
            places = [(i + n, rows[n](k)) for n in range(3)]
            band[i, k * 128 : k * 128 + 16, c : c + 128] = edge_band(places, 0)
            band[i, k * 128 + 16 : k * 128 + 112, c : c + 128] = jnp.zeros((96, 128), BF)
            band[i, k * 128 + 112 : k * 128 + 128, c : c + 128] = edge_band(places, 112)

    def of(taps, i):
        return lambda k: taps[3 * i + k : 3 * i + k + 1]

    taps = tap_rows(quad, lato, lono, 1)
    fwd = [one_tap(taps, a) for a in range(3)]
    put_bands(bandf, 0, [of(fwd[0] * top, 0), of(fwd[1], 0), of(fwd[2], 0)])
    put_bands(bandf, 1, [of(fwd[0], 1), of(fwd[1], 1), of(fwd[2] * bottom, 1)])
    pl.semaphore_wait(tok.at[0], 5)
    two = (e, l, (x + 2) % 4), ((1 - yh) * 2 + core, l, x), z_device((z + 1) % 16), z_device((z + 15) % 16)
    for device in two:
        signal(tok.at[1], device)
    for c in first[2]:
        c.wait_recv()
    adj = [one_tap(adjoint, a) for a in range(3)]
    put_bands(banda, 0, [of(one_tap(brecv[0], 2) * top, 1), of(adj[1], 0), of(adj[0], 1)])
    put_bands(banda, 1, [of(adj[2], 0), of(adj[1], 1), of(one_tap(brecv[1], 0) * bottom, 0)])

    def spread(band, ext, f, out):
        for i in range(2):
            cells = ext[f, i : i + 4].reshape(512, 256)
            got = dot(band[i], cells, 1, 0).astype(BF)
            for k in range(3):
                out[k, i * 128 : i * 128 + 128] = got[k * 128 : k * 128 + 128]

    def mixed(spreaded, weight, cw):
        total = dot(spreaded[0], weight[0], 1, cw)
        for k in range(1, 3):
            total = total + dot(spreaded[k], weight[k], 1, cw)
        return total

    loads[5].wait()
    loads[6].wait()
    for c in first[0]:
        c.wait_recv()
    spread(bandf, ext1, 0, u_ref)
    hidden = mixed(u_ref, w1_ref, 1)
    root = math.sqrt(2.0 / math.pi)
    square = hidden * hidden
    bend = jnp.tanh(root * hidden * (1.0 + 0.044715 * square))
    act = (0.5 * hidden * (1.0 + bend)).astype(BF)
    slope[...] = 0.5 * (1.0 + bend) + (0.5 * root) * hidden * (1.0 - bend * bend) * (1.0 + (3 * 0.044715) * square)
    ext2[0, 1:3] = act.reshape(2, 4, 32, 256)

    for c in first[1]:
        c.wait_recv()
    spread(banda, ext1, 1, t_ref)

    def put_grad(ch, row, value):
        value = value.astype(BF)
        gs[ch, 0, row : row + 256] = value[:, :128]
        gs[ch, 1, row : row + 256] = value[:, 128:]

    cores = [
        copy_to(gs.at[ch, 1 - core], crecv.at[ch], sc.at[ch], rc.at[ch], partner) for ch in range(2)
    ]
    for k in range(3):
        put_grad(0, k * 256, dot(t_ref[k], act, 0, 0))
    cores[0].start()
    act_grad = mixed(t_ref, w2_ref, 0).astype(BF).astype(F32)
    hid_grad = (act_grad * slope[...]).astype(BF)
    ext2[1, 1:3] = hid_grad.reshape(2, 4, 32, 256)
    for k in range(3):
        put_grad(1, k * 256, dot(hid_grad, u_ref[k], 0, 0))
    cores[1].start()
    pl.semaphore_wait(tok.at[1], 4)
    for d in (2, 14):
        signal(tok.at[2], z_device((z + d) % 16))

    def piece(ch, s):
        peer, device = xy_peer(s)
        rows = pl.ds(pl.multiple_of(peer * PIECE, 16), PIECE)
        return copy_to(xs.at[ch, rows], xrecv.at[ch, s - 1], sx.at[ch, s - 1], rx.at[ch, s - 1], device)

    for ch in range(2):
        cores[ch].wait_recv()
        xs[ch] = (gs[ch, core].astype(F32) + crecv[ch].astype(F32)).astype(BF)

        def send_piece(s, c, ch=ch):
            piece(ch, far_first(s)).start()
            return c

        lax.fori_loop(0, 15, send_piece, 0)

    pl.semaphore_wait(tok.at[2], 2)
    for d in (4, 12):
        signal(tok.at[3], z_device((z + d) % 16))

    mine = pl.ds(pl.multiple_of(me * PIECE, 16), PIECE)

    def near(ch, s):
        return copy_to(zrecv.at[ch, p], zrecv.at[ch, p], sz.at[ch, s - 1], rz.at[ch, p], z_device(grp * 4 + (p + s) % 4))

    def near_in(ch, s):
        q = (p + s) % 4
        return copy_to(zrecv.at[ch, q], zrecv.at[ch, q], sz.at[ch, s - 1], rz.at[ch, q], z_device(grp * 4 + q))

    for ch in range(2):

        def add_piece(s, total, ch=ch):
            piece(ch, s).wait_recv()
            return total + xrecv[ch, s - 1].astype(F32)

        zrecv[ch, p] = lax.fori_loop(1, 16, add_piece, xs[ch, mine].astype(F32)).astype(BF)
        for s in range(1, 4):
            near(ch, s).start()

    second = [c for f in range(2) for c in rows(ext2, f, s2, r2, 8 * f) + edges(ext2, f, s2, r2, 8 * f + 2)]
    for c in second:
        c.start()

    def far(ch, n, group, member):
        return copy_to(
            zgroup.at[ch, grp], zgroup.at[ch, grp], sf.at[ch, n], rf.at[ch, grp], z_device(group * 4 + member)
        )

    before, after, opposite = (grp + 3) % 4, (grp + 1) % 4, (grp + 2) % 4
    to_left = [(opposite, 2), (opposite, 3), (before, 0), (before, 1), (before, 2), (before, 3)]
    to_right = [(opposite, 1), (opposite, 0), (after, 3), (after, 2), (after, 1), (after, 0)]

    def all_four(ref):
        total = ref[0].astype(F32)
        for q in range(1, 4):
            total = total + ref[q].astype(F32)
        return total.astype(BF)

    pl.semaphore_wait(tok.at[3], 2)
    for ch in range(2):
        for s in range(1, 4):
            near_in(ch, s).wait_recv()
        zgroup[ch, grp] = all_four(zrecv.at[ch])

        @pl.when(p == 0)
        def _(ch=ch):
            for n in range(6):
                far(ch, n, *to_left[n]).start()

        @pl.when(p == 3)
        def _(ch=ch):
            for n in range(6):
                far(ch, n, *to_right[n]).start()

    def spread_piece(ch, s):
        cells = fin.at[ch, core, mine]
        return copy_to(cells, cells, sa.at[ch, s - 1], ra.at[ch, s - 1], xy_peer(s)[1])

    for ch in range(2):
        for s in range(1, 4):
            q = (grp + s) % 4
            cells = zgroup.at[ch, q]
            copy_to(cells, cells, sf.at[ch, 0], rf.at[ch, q], z_device(q * 4)).wait_recv()
        fin[ch, core, mine] = all_four(zgroup.at[ch])

        def send_back(s, c, ch=ch):
            spread_piece(ch, far_first(s)).start()
            return c

        lax.fori_loop(0, 15, send_back, 0)

    def turned_back(cells, out):
        for h in range(2):
            lanes = slice(h * 128, h * 128 + 128)
            both = jnp.concatenate([cells[0:128, lanes], cells[128:256, lanes]], axis=1)
            out[h * 256 : h * 256 + 256] = dot(sel[...], both, 1, 1).astype(BF)

    for c in second:
        c.wait_recv()
    spread(bandf, ext2, 0, u_ref)
    turned_back(mixed(u_ref, w2_ref, 1).astype(BF), lo_ref)
    spread(banda, ext2, 1, t_ref)
    turned_back(mixed(t_ref, w1_ref, 0).astype(BF), sg_ref)

    for c in first[0] + first[1] + first[2] + second + cores:
        c.wait_send()
    for ch in range(2):

        def wait_sent(s, c, ch=ch):
            piece(ch, s).wait_send()
            return c

        lax.fori_loop(1, 16, wait_sent, 0)
        for s in range(1, 4):
            near(ch, s).wait_send()

        @pl.when(p == 0)
        def _(ch=ch):
            for n in range(6):
                far(ch, n, *to_left[n]).wait_send()

        @pl.when(p == 3)
        def _(ch=ch):
            for n in range(6):
                far(ch, n, *to_right[n]).wait_send()

    swaps = [copy_to(fin.at[ch, core], fin.at[ch, core], sd.at[ch], rd.at[ch], partner) for ch in range(2)]
    for ch in range(2):

        def wait_back(s, c, ch=ch):
            spread_piece(ch, s).wait()
            return c

        lax.fori_loop(1, 16, wait_back, 0)
        swaps[ch].start()
    for c in swaps:
        c.wait()


def finish(lo_ref, sg_ref, fin, lo_hbm, sg_hbm, d1_hbm, d2_hbm, d_ref, sems):
    stores = [
        pltpu.make_async_copy(lo_ref, lo_hbm, sems.at[6]),
        pltpu.make_async_copy(sg_ref, sg_hbm, sems.at[7]),
    ]
    scale = 1.0 / math.sqrt(4 * 64 * 512)
    for n in range(2):
        for k in range(3):
            for h in range(2):
                rows = slice(k * 256, k * 256 + 256)
                d_ref[n, k, :, h * 128 : h * 128 + 128] = fin[n, h, rows].astype(F32) * scale
            stores.append(pltpu.make_async_copy(d_ref.at[n, k], (d2_hbm, d1_hbm)[n].at[k], sems.at[3 * n + k]))
            stores[-1].start()
    stores[0].start()
    stores[1].start()
    for c in stores:
        c.wait()


def body(state_field, first_weight, second_weight, quadrature, lat_offsets, lon_offsets, cotangent):
    vmem = pl.BlockSpec(memory_space=pltpu.VMEM)
    anywhere = pl.BlockSpec(memory_space=pl.ANY)
    dma = pltpu.SemaphoreType.DMA
    lo, sg, fin = pl.pallas_call(
        kernel,
        out_shape=(
            pltpu.VMEM((512, 128), BF),
            pltpu.VMEM((512, 128), BF),
            pltpu.VMEM((2, 2, 768, 128), BF),
        ),
        in_specs=[anywhere] * 7,
        out_specs=[vmem] * 3,
        scratch_shapes=[
            pltpu.VMEM((2, 512, 128), BF),
            pltpu.VMEM((3, 256, 256), BF),
            pltpu.VMEM((3, 256, 256), BF),
            pltpu.VMEM((3, 2, 12), F32),
            pltpu.VMEM((3, 2, 12), jnp.int32),
            pltpu.VMEM((3, 2, 12), jnp.int32),
            pltpu.VMEM((256, 256), BF),
            pltpu.VMEM((2, 5, 4, 32, 256), BF),
            pltpu.VMEM((2, 5, 4, 32, 256), BF),
            pltpu.VMEM((8, 128), F32),
            pltpu.VMEM((2, 8, 128), F32),
            pltpu.VMEM((2, 384, 512), BF),
            pltpu.VMEM((2, 384, 512), BF),
            pltpu.VMEM((3, 256, 256), BF),
            pltpu.VMEM((3, 256, 256), BF),
            pltpu.VMEM((256, 256), F32),
            pltpu.VMEM((2, 2, 768, 128), BF),
            pltpu.VMEM((2, 768, 128), BF),
            pltpu.VMEM((2, 768, 128), BF),
            pltpu.VMEM((2, 15, PIECE, 128), BF),
            pltpu.VMEM((2, 4, PIECE, 128), BF),
            pltpu.VMEM((2, 4, PIECE, 128), BF),
            dma((7,)),
            dma((18,)), dma((18,)),
            dma((16,)), dma((16,)),
            dma((2,)), dma((2,)),
            dma((2, 15)), dma((2, 15)),
            dma((2, 3)), dma((2, 4)),
            dma((2, 6)), dma((2, 4)),
            dma((2, 15)), dma((2, 15)),
            dma((2,)), dma((2,)),
            pltpu.SemaphoreType.REGULAR((4,)),
        ],
        compiler_params=pltpu.CompilerParams(collective_id=0, has_side_effects=True, vmem_limit_bytes=60 * 2**20),
        cost_estimate=pl.CostEstimate(flops=1_500_000_000, bytes_accessed=4_000_000, transcendentals=65536),
        name="conv_pair",
    )(
        state_field.reshape(512, 128),
        cotangent.reshape(512, 128),
        first_weight,
        second_weight,
        *(jnp.transpose(t, (1, 0, 2)) for t in (quadrature, lat_offsets, lon_offsets)),
    )
    lo, sg, d1, d2 = pl.pallas_call(
        finish,
        out_shape=(
            jax.ShapeDtypeStruct((512, 128), BF),
            jax.ShapeDtypeStruct((512, 128), BF),
            jax.ShapeDtypeStruct((3, 256, 256), F32),
            jax.ShapeDtypeStruct((3, 256, 256), F32),
        ),
        in_specs=[vmem] * 3,
        out_specs=[anywhere] * 4,
        scratch_shapes=[pltpu.VMEM((2, 3, 256, 256), F32), dma((8,))],
        compiler_params=pltpu.CompilerParams(vmem_limit_bytes=4 * 2**20),
        name="put_out",
    )(lo, sg, fin)
    return lo.reshape(1, 256, 2, 128), sg.reshape(1, 256, 2, 128), d1, d2


def solution(mesh):
    in_specs = (
        P("ens", None, "lat", "lon"),
        P(),
        P(),
        P("lat", None, None),
        P("lat", None, None),
        P("lat", None, None),
        P("ens", None, "lat", "lon"),
    )
    out_specs = (P("ens", None, "lat", "lon"), P("ens", None, "lat", "lon"), P(), P())
    return jax.shard_map(body, mesh=mesh, in_specs=in_specs, out_specs=out_specs, check_vma=False)
```

time: 58 us -> 56.3 us (0.971)
  Pallas kernels: 57.2 us -> 55.6 us
    pallas_call x1, Pallas kernels: 2.29 us -> 1.32 us  [body(): pl.pallas_call(finish, out_shape=(jax.ShapeDtypeStruct((512, 128), BF), j...]
    pallas_call x1, Pallas kernels: 54.9 us -> 54.2 us  [body(): pl.pallas_call(kernel, out_shape=(pltpu.VMEM((512, 128), BF), pltpu.VMEM(...]
where the time goes in v3:
time: 56.3 us; the launch traced here: 56.2 us
  Pallas kernels  55.6 us (99%)
  between operations  0.64 us (1%)
    pallas_call x1, Pallas kernels, body(): pl.pallas_call(kernel, out_shape=(pltpu.VMEM((512, 128), BF), pltpu.VMEM(...  54.2 us
    pallas_call x1, Pallas kernels, body(): pl.pallas_call(finish, out_shape=(jax.ShapeDtypeStruct((512, 128), BF), j...  1.32 us

profile of v3, /device:TPU:1, one launch (start us, length us, event | category | flops | bytes accessed | tf_op | source)
XLA Modules:
  0.0 56.2 jit_solution(14194554441726533008)
XLA Ops:
  0.6 54.2 %conv_pair.1 = (bf16[512,128]{1,0:T(8,128)(2,1)S(1)}, bf16[512,128]{1,0:T(8,128)(2,1)S(1)}, bf16[2,2,768,128]{3,2,1,0:T(8,128)(2,1)S(1)}) custom-call(bf16[512,128]{1,0:T(8,128)(2,1)} %bitcast.7, bf16[512,128]{1,0:T(8,128)(2,1)} %bitcast.8, bf16[3,256,256]{2,1,0:T(8,128)(2,1)} %w1_hbm.1, bf16[3,256,256]{2,1,0:T(8,128)(2,1)} %w2_hbm.1, f32[3,2,12]{2,1,0:T(2,128)} %bitcast.11, ...), custom_call_target="tpu_custom_call" | custom-call | flops 1500000000 | bytes 4000000 | tf_op jit(solution)/shard_map/conv_pair/pallas_call | solution.py:418
  54.9 1.3 %put_out.1 = (bf16[512,128]{1,0:T(8,128)(2,1)}, bf16[512,128]{1,0:T(8,128)(2,1)}, f32[3,256,256]{2,1,0:T(8,128)}, f32[3,256,256]{2,1,0:T(8,128)}) custom-call(bf16[512,128]{1,0:T(8,128)(2,1)S(1)} %get-tuple-element.11.lo_ref, bf16[512,128]{1,0:T(8,128)(2,1)S(1)} %get-tuple-element.12.sg_ref, bf16[2,2,768,128]{3,2,1,0:T(8,128)(2,1)S(1)} %get-tuple-element.13.fin), custom_call_target="tpu_custom_call" | custom-call | tf_op jit(solution)/shard_map/put_out/pallas_call | solution.py:471

commit v4 on v3

--- a/solution.py
+++ b/solution.py
@@ -105,8 +105,8 @@
             )
         )
     ]
-    for c in loads:
-        c.start()
+    for n in (1, 2, 3, 0, 4, 5, 6):
+        loads[n].start()
 
     barrier = pltpu.get_barrier_semaphore()
 
@@ -151,15 +151,6 @@
             copy_to(bsend, brecv.at[0], s1.at[17], r1.at[17], (e, down, x)),
         ]
     )
-    loads[0].wait()
-    turn(0)
-    pl.semaphore_wait(barrier, 10)
-    for c in first[0]:
-        c.start()
-    loads[4].wait()
-    turn(1)
-    for c in first[1]:
-        c.start()
     for n in (1, 2, 3):
         loads[n].wait()
     pad = jnp.zeros((2, 12), jnp.int32)
@@ -168,7 +159,16 @@
     quad = jnp.concatenate([quad_ref[:, 0], quad_ref[:, 1], pad.astype(F32)])
     adjoint = tap_rows(quad, lato, lono, -1)
     bsend[...] = adjoint
+    loads[0].wait()
+    turn(0)
+    pl.semaphore_wait(barrier, 10)
     for c in first[2]:
+        c.start()
+    for c in first[0]:
+        c.start()
+    loads[4].wait()
+    turn(1)
+    for c in first[1]:
         c.start()
     for device in ((e, up, x), (e, down, x), (e, l, left), (e, l, right), across):
         signal(tok.at[0], device)
@@ -229,6 +229,9 @@
     slope[...] = 0.5 * (1.0 + bend) + (0.5 * root) * hidden * (1.0 - bend * bend) * (1.0 + (3 * 0.044715) * square)
     ext2[0, 1:3] = act.reshape(2, 4, 32, 256)
 
+    pl.semaphore_wait(tok.at[1], 4)
+    for d in (2, 14):
+        signal(tok.at[2], z_device((z + d) % 16))
     for c in first[1]:
         c.wait_recv()
     spread(banda, ext1, 1, t_ref)
@@ -250,9 +253,9 @@
     for k in range(3):
         put_grad(1, k * 256, dot(hid_grad, u_ref[k], 0, 0))
     cores[1].start()
-    pl.semaphore_wait(tok.at[1], 4)
-    for d in (2, 14):
-        signal(tok.at[2], z_device((z + d) % 16))
+    pl.semaphore_wait(tok.at[2], 2)
+    for d in (4, 12):
+        signal(tok.at[3], z_device((z + d) % 16))
 
     def piece(ch, s):
         peer, device = xy_peer(s)
@@ -269,10 +272,6 @@
 
         lax.fori_loop(0, 15, send_piece, 0)
 
-    pl.semaphore_wait(tok.at[2], 2)
-    for d in (4, 12):
-        signal(tok.at[3], z_device((z + d) % 16))
-
     mine = pl.ds(pl.multiple_of(me * PIECE, 16), PIECE)
 
     def near(ch, s):
@@ -293,8 +292,6 @@
             near(ch, s).start()
 
     second = [c for f in range(2) for c in rows(ext2, f, s2, r2, 8 * f) + edges(ext2, f, s2, r2, 8 * f + 2)]
-    for c in second:
-        c.start()
 
     def far(ch, n, group, member):
         return copy_to(
@@ -326,6 +323,9 @@
         def _(ch=ch):
             for n in range(6):
                 far(ch, n, *to_right[n]).start()
+
+    for c in second:
+        c.start()
 
     def spread_piece(ch, s):
         cells = fin.at[ch, core, mine]

time: 56.3 us -> 54.6 us (0.970)
  Pallas kernels: 55.6 us -> 53.8 us
    pallas_call x1, Pallas kernels: 54.2 us -> 52.5 us  [body(): pl.pallas_call(kernel, out_shape=(pltpu.VMEM((512, 128), BF), pltpu.VMEM(...]
where the time goes in v4:
time: 54.6 us; the launch traced here: 54.5 us
  Pallas kernels  53.8 us (99%)
  between operations  0.64 us (1%)
    pallas_call x1, Pallas kernels, body(): pl.pallas_call(kernel, out_shape=(pltpu.VMEM((512, 128), BF), pltpu.VMEM(...  52.5 us
    pallas_call x1, Pallas kernels, body(): pl.pallas_call(finish, out_shape=(jax.ShapeDtypeStruct((512, 128), BF), j...  1.32 us

profile of v4, /device:TPU:1, one launch (start us, length us, event | category | flops | bytes accessed | tf_op | source)
XLA Modules:
  0.0 54.5 jit_solution(1444688338007801493)
XLA Ops:
  0.6 52.5 %conv_pair.1 = (bf16[512,128]{1,0:T(8,128)(2,1)S(1)}, bf16[512,128]{1,0:T(8,128)(2,1)S(1)}, bf16[2,2,768,128]{3,2,1,0:T(8,128)(2,1)S(1)}) custom-call(bf16[512,128]{1,0:T(8,128)(2,1)} %bitcast.7, bf16[512,128]{1,0:T(8,128)(2,1)} %bitcast.8, bf16[3,256,256]{2,1,0:T(8,128)(2,1)} %w1_hbm.1, bf16[3,256,256]{2,1,0:T(8,128)(2,1)} %w2_hbm.1, f32[3,2,12]{2,1,0:T(2,128)} %bitcast.11, ...), custom_call_target="tpu_custom_call" | custom-call | flops 1500000000 | bytes 4000000 | tf_op jit(solution)/shard_map/conv_pair/pallas_call | solution.py:418
  53.2 1.3 %put_out.1 = (bf16[512,128]{1,0:T(8,128)(2,1)}, bf16[512,128]{1,0:T(8,128)(2,1)}, f32[3,256,256]{2,1,0:T(8,128)}, f32[3,256,256]{2,1,0:T(8,128)}) custom-call(bf16[512,128]{1,0:T(8,128)(2,1)S(1)} %get-tuple-element.11.lo_ref, bf16[512,128]{1,0:T(8,128)(2,1)S(1)} %get-tuple-element.12.sg_ref, bf16[2,2,768,128]{3,2,1,0:T(8,128)(2,1)S(1)} %get-tuple-element.13.fin), custom_call_target="tpu_custom_call" | custom-call | tf_op jit(solution)/shard_map/put_out/pallas_call | solution.py:471

commit v5 on v4

--- a/solution.py
+++ b/solution.py
@@ -344,6 +344,16 @@
 
         lax.fori_loop(0, 15, send_back, 0)
 
+    swaps = [copy_to(fin.at[ch, core], fin.at[ch, core], sd.at[ch], rd.at[ch], partner) for ch in range(2)]
+    for ch in range(2):
+
+        def wait_back(s, c, ch=ch):
+            spread_piece(ch, s).wait()
+            return c
+
+        lax.fori_loop(1, 16, wait_back, 0)
+        swaps[ch].start()
+
     def turned_back(cells, out):
         for h in range(2):
             lanes = slice(h * 128, h * 128 + 128)
@@ -378,16 +388,6 @@
         def _(ch=ch):
             for n in range(6):
                 far(ch, n, *to_right[n]).wait_send()
-
-    swaps = [copy_to(fin.at[ch, core], fin.at[ch, core], sd.at[ch], rd.at[ch], partner) for ch in range(2)]
-    for ch in range(2):
-
-        def wait_back(s, c, ch=ch):
-            spread_piece(ch, s).wait()
-            return c
-
-        lax.fori_loop(1, 16, wait_back, 0)
-        swaps[ch].start()
     for c in swaps:
         c.wait()
 

time: 54.6 us -> 54.4 us (level)
  no operation moved by 1% of the time
where the time goes in v5:
time: 54.4 us; the launch traced here: 54.2 us
  Pallas kernels  53.6 us (99%)
  between operations  0.64 us (1%)
    pallas_call x1, Pallas kernels, body(): pl.pallas_call(kernel, out_shape=(pltpu.VMEM((512, 128), BF), pltpu.VMEM(...  52.3 us
    pallas_call x1, Pallas kernels, body(): pl.pallas_call(finish, out_shape=(jax.ShapeDtypeStruct((512, 128), BF), j...  1.32 us

profile of v5, /device:TPU:1, one launch (start us, length us, event | category | flops | bytes accessed | tf_op | source)
XLA Modules:
  0.0 54.2 jit_solution(13583078504773071851)
XLA Ops:
  0.6 52.3 %conv_pair.1 = (bf16[512,128]{1,0:T(8,128)(2,1)S(1)}, bf16[512,128]{1,0:T(8,128)(2,1)S(1)}, bf16[2,2,768,128]{3,2,1,0:T(8,128)(2,1)S(1)}) custom-call(bf16[512,128]{1,0:T(8,128)(2,1)} %bitcast.7, bf16[512,128]{1,0:T(8,128)(2,1)} %bitcast.8, bf16[3,256,256]{2,1,0:T(8,128)(2,1)} %w1_hbm.1, bf16[3,256,256]{2,1,0:T(8,128)(2,1)} %w2_hbm.1, f32[3,2,12]{2,1,0:T(2,128)} %bitcast.11, ...), custom_call_target="tpu_custom_call" | custom-call | flops 1500000000 | bytes 4000000 | tf_op jit(solution)/shard_map/conv_pair/pallas_call | solution.py:418
  52.9 1.3 %put_out.1 = (bf16[512,128]{1,0:T(8,128)(2,1)}, bf16[512,128]{1,0:T(8,128)(2,1)}, f32[3,256,256]{2,1,0:T(8,128)}, f32[3,256,256]{2,1,0:T(8,128)}) custom-call(bf16[512,128]{1,0:T(8,128)(2,1)S(1)} %get-tuple-element.11.lo_ref, bf16[512,128]{1,0:T(8,128)(2,1)S(1)} %get-tuple-element.12.sg_ref, bf16[2,2,768,128]{3,2,1,0:T(8,128)(2,1)S(1)} %get-tuple-element.13.fin), custom_call_target="tpu_custom_call" | custom-call | tf_op jit(solution)/shard_map/put_out/pallas_call | solution.py:471

commit v6 on v5

--- a/solution.py
+++ b/solution.py
@@ -293,6 +293,9 @@
 
     second = [c for f in range(2) for c in rows(ext2, f, s2, r2, 8 * f) + edges(ext2, f, s2, r2, 8 * f + 2)]
 
+    for c in second:
+        c.start()
+
     def far(ch, n, group, member):
         return copy_to(
             zgroup.at[ch, grp], zgroup.at[ch, grp], sf.at[ch, n], rf.at[ch, grp], z_device(group * 4 + member)
@@ -323,9 +326,6 @@
         def _(ch=ch):
             for n in range(6):
                 far(ch, n, *to_right[n]).start()
-
-    for c in second:
-        c.start()
 
     def spread_piece(ch, s):
         cells = fin.at[ch, core, mine]

time: 54.4 us -> 55.7 us (1.024)
  Pallas kernels: 53.6 us -> 54.9 us
    pallas_call x1, Pallas kernels: 52.3 us -> 53.6 us  [body(): pl.pallas_call(kernel, out_shape=(pltpu.VMEM((512, 128), BF), pltpu.VMEM(...]
where the time goes in v6:
time: 55.7 us; the launch traced here: 55.6 us
  Pallas kernels  54.9 us (99%)
  between operations  0.64 us (1%)
    pallas_call x1, Pallas kernels, body(): pl.pallas_call(kernel, out_shape=(pltpu.VMEM((512, 128), BF), pltpu.VMEM(...  53.6 us
    pallas_call x1, Pallas kernels, body(): pl.pallas_call(finish, out_shape=(jax.ShapeDtypeStruct((512, 128), BF), j...  1.32 us

profile of v6, /device:TPU:1, one launch (start us, length us, event | category | flops | bytes accessed | tf_op | source)
XLA Modules:
  0.0 55.6 jit_solution(4728766351801623528)
XLA Ops:
  0.6 53.6 %conv_pair.1 = (bf16[512,128]{1,0:T(8,128)(2,1)S(1)}, bf16[512,128]{1,0:T(8,128)(2,1)S(1)}, bf16[2,2,768,128]{3,2,1,0:T(8,128)(2,1)S(1)}) custom-call(bf16[512,128]{1,0:T(8,128)(2,1)} %bitcast.7, bf16[512,128]{1,0:T(8,128)(2,1)} %bitcast.8, bf16[3,256,256]{2,1,0:T(8,128)(2,1)} %w1_hbm.1, bf16[3,256,256]{2,1,0:T(8,128)(2,1)} %w2_hbm.1, f32[3,2,12]{2,1,0:T(2,128)} %bitcast.11, ...), custom_call_target="tpu_custom_call" | custom-call | flops 1500000000 | bytes 4000000 | tf_op jit(solution)/shard_map/conv_pair/pallas_call | solution.py:418
  54.3 1.3 %put_out.1 = (bf16[512,128]{1,0:T(8,128)(2,1)}, bf16[512,128]{1,0:T(8,128)(2,1)}, f32[3,256,256]{2,1,0:T(8,128)}, f32[3,256,256]{2,1,0:T(8,128)}) custom-call(bf16[512,128]{1,0:T(8,128)(2,1)S(1)} %get-tuple-element.11.lo_ref, bf16[512,128]{1,0:T(8,128)(2,1)S(1)} %get-tuple-element.12.sg_ref, bf16[2,2,768,128]{3,2,1,0:T(8,128)(2,1)S(1)} %get-tuple-element.13.fin), custom_call_target="tpu_custom_call" | custom-call | tf_op jit(solution)/shard_map/put_out/pallas_call | solution.py:471
